TPU v7x, 32 devices: a whole 2x2x4 slice. The times are simulated.
32 devices in a mesh: dp: 4 (over y, core), fsdp: 8 (over z, x).
Axes of the slice: x: 2, y: 2, z: 4, core: 2. Of those that a mesh axis runs over, the one named last changes fastest.
Arguments:
- patches: bfloat16 [32, 768, 768], P(('dp', 'fsdp')), may hold values from -6 to 6
- positions: int32 [32, 768], P(('dp', 'fsdp')), may hold values from 0 to 198, as said below
- segments: int32 [32, 768], P(('dp', 'fsdp')), may hold values from 0 to 15, as said below
- labels: int32 [32, 15], P(('dp', 'fsdp')), may hold values from 0 to 999
- teacher: int32 [32, 15], P(('dp', 'fsdp')), may hold values from 0 to 999
- layer_master: float32 [2, 1802240], P(None, ('dp', 'fsdp'))
- layer_moment: float32 [2, 1802240], P(None, ('dp', 'fsdp'))
- layer_second: float32 [2, 1802240], P(None, ('dp', 'fsdp'))
- global_master: float32 [1146880], P(('dp', 'fsdp'))
- global_moment: float32 [1146880], P(('dp', 'fsdp'))
- global_second: float32 [1146880], P(('dp', 'fsdp'))
Outputs:
- new_layer_master: float32 [2, 1802240], P(None, ('dp', 'fsdp'))
- new_layer_moment: float32 [2, 1802240], P(None, ('dp', 'fsdp'))
- new_layer_second: float32 [2, 1802240], P(None, ('dp', 'fsdp'))
- new_global_master: float32 [1146880], P(('dp', 'fsdp'))
- new_global_moment: float32 [1146880], P(('dp', 'fsdp'))
- new_global_second: float32 [1146880], P(('dp', 'fsdp'))
- grad_norm: float32 [], replicated
- loss_sum: float32 [], replicated
Inputs may be any that keep to these rules, and one draw needn't show every extreme that they name: `positions`: in each sequence 15 images of 51 tokens stand in order, with the remaining tokens as padding before, between or after them; an image's first token has position 196, its second 196 + 1, the others rows of the 14 x 14 table in a 7 x 7 window, row by row; padding has position 198. `segments`: the number of a token's image in its sequence, counting from 0 in order; padding tokens have 15.
All inputs are finite; a program needn't handle non-finite values.
Results may differ from a plain program's by a relative error of at most 0.012.
Values may be sent and summed in bfloat16 or wider, within the bound.
A program may use at most 192 MiB of HBM per device.

v0:
```python
import functools

import jax
import jax.numpy as jnp
from jax import lax
from jax.experimental import pallas as pl
from jax.experimental.pallas import tpu as pltpu
from jax.sharding import PartitionSpec as P

D = 384
HEADS = 6
HEAD_DIM = 64
FF = 1536
CLASSES = 1000
PATCH = 768
TABLE = 196
IMAGES = 15
SEQ = 768
STEP = 10
LANES = 128
PARTS = 32

NORM_EPS = 1e-06
BETA_ONE = 0.9
BETA_TWO = 0.999
ADAM_EPS = 1e-08
LEARN_RATE = 0.1
WEIGHT_DECAY = 0.05
CLIP_NORM = 0.01
MASK_FILL = -1000000000.0
SCORE_SCALE = HEAD_DIM ** (-0.5)
LOW = jnp.bfloat16
FULL = jnp.float32
HIGHEST = lax.Precision.HIGHEST

QKV_AT, PROJ_AT, FC1_AT, FC2_AT = 0, 3456, 4608, 9216
PRE_GAIN_AT, PRE_BIAS_AT, QUERY_BIAS_AT, VALUE_BIAS_AT = 13824, 13827, 13830, 13833
PROJ_BIAS_AT, MID_GAIN_AT, MID_BIAS_AT, FC1_BIAS_AT, FC2_BIAS_AT = 13836, 13839, 13842, 13845, 13857
LAYER_END = 13860
PATCH_AT, POS_AT, PATCH_BIAS_AT, FINAL_GAIN_AT, FINAL_BIAS_AT = 0, 2304, 2898, 2901, 2904
HEAD_AT, HEAD_BIAS_AT, GLOBAL_END = 2907, 8907, 8923
GROUP, GROUP_ROWS, GROUPS = 8, 125, 48
HEAD_LANES = 2048
PICKED = 32
WINDOWS, WINDOW = 8, 128
ROWS = 256
LAYER_ROWS, GLOBAL_ROWS = 440, 280


def dot(a, b, dims=(1, 0), precision=None):
    return lax.dot_general(
        a, b, (((dims[0],), (dims[1],)), ((), ())), precision=precision, preferred_element_type=FULL
    )


def dot_nt(a, b, precision=None):
    return dot(a, b, (1, 1), precision)


def dot_tn(a, b, precision=None):
    return dot(a, b, (0, 0), precision)


def row_mean(x):
    return jnp.sum(x, axis=-1, keepdims=True) * (1.0 / D)


def normalise(x):
    center = x - row_mean(x)
    inverse = lax.rsqrt(row_mean(center * center) + NORM_EPS)
    return center * inverse, inverse


def norm_back(grad, gain, unit, inverse):
    scaled = grad * gain
    return inverse * (scaled - row_mean(scaled) - unit * row_mean(scaled * unit))


def col_sum(x):
    return jnp.sum(x.astype(FULL), axis=0, keepdims=True)


def gelu_parts(x):
    size = jnp.abs(x)
    bell = jnp.exp(-0.5 * x * x)
    base = 1.0 + (0.3275911 * 0.7071067811865476) * size
    t = pl.reciprocal(base, approx=True)
    t = t * (2.0 - base * t)
    tail = ((((1.061405429 * t - 1.453152027) * t + 1.421413741) * t - 0.284496736) * t + 0.254829592) * t
    tail = 0.5 * tail * bell
    phi = jnp.where(x < 0, tail, 1.0 - tail)
    return x * phi, phi + x * (bell * 0.3989422804014327)


def step_kernel(
    loss_scale,
    pat, pos, seg, lab, tea, a0, a1, ag,
    g0, g1, gg, loss,
    b0, b1, bg, flat, flatg, wqkv, wproj, wfc1, wfc2, wpat, wpos, whead, vecs,
    pos_col, seg_col, unit_a, inv_a, h_a, unit_b, inv_b, h_b, qkv, probs, att, attl, x0, x1, dgelu, act, gpre,
    kv, low, sems,
):
    head_of_lane = lax.broadcasted_iota(jnp.int32, (1, LANES), 1) // HEAD_DIM

    loads = [
        pltpu.make_async_copy(src, dst, sems.at[i]) for i, (src, dst) in enumerate(((ag, bg), (a0, b0), (a1, b1)))
    ]
    for load in loads:
        load.start()

    def spread(buf, flat, rows):
        def one(s, carry):
            flat[pl.ds(pl.multiple_of(s * rows, 8), rows), :] = buf[s, :rows, :].astype(FULL)
            return carry

        lax.fori_loop(0, PARTS, one, 0)

    def gather_rows(buf, flat, rows):
        def one(s, carry):
            buf[s, :rows, :] = flat[pl.ds(pl.multiple_of(s * rows, 8), rows), :].astype(LOW)
            return carry

        lax.fori_loop(0, PARTS, one, 0)

    def take(flat, dst, at, rows, width):
        count = width // LANES

        def one(c, carry):
            value = flat[pl.ds(at + c, rows, stride=count), :].astype(LOW)
            dst[:rows, pl.ds(pl.multiple_of(c * LANES, LANES), LANES)] = value
            return carry

        lax.fori_loop(0, count, one, 0)

    def take_row(flat, at, width):
        return jnp.concatenate([flat[at + i : at + i + 1, :] for i in range(width // LANES)], axis=1)

    def put_row(at, value, flat=flat):
        for i in range(value.shape[1] // LANES):
            flat[at + i : at + i + 1, :] = value[:, i * LANES : (i + 1) * LANES]

    def put(at, start, width, value, first=0, flat=flat):
        count = width // LANES
        rows = value.shape[0]
        for i in range(value.shape[1] // LANES):
            flat[pl.ds(at + start * count + first + i, rows, stride=count), :] = value[:, i * LANES : (i + 1) * LANES]

    for i in range(SEQ // LANES):
        lanes = slice(i * LANES, (i + 1) * LANES)
        for src, dst in ((pos, pos_col), (seg, seg_col)):
            dst[lanes, :] = jnp.transpose(jnp.broadcast_to(src[0:1, lanes].astype(FULL), (LANES, LANES)))
    pos_row = pos[0:1, :]
    seg_row = seg[0:1, :]
    picked_row = lax.broadcasted_iota(jnp.int32, (PICKED, 1), 0)
    picked_image = jnp.where(picked_row < IMAGES, picked_row, picked_row - IMAGES)
    picked_image = jnp.where(picked_row < 2 * IMAGES, picked_image, -1)
    picked_place = jnp.where(picked_row < IMAGES, TABLE, TABLE + 1)
    picker = ((seg_row == picked_image) & (pos_row == picked_place)).astype(FULL)
    picker_low = picker.astype(LOW)

    loads[0].wait()
    spread(bg, flatg, GLOBAL_ROWS)
    take(flatg, wpat, PATCH_AT, PATCH, D)
    take(flatg, wpos, POS_AT, TABLE + 2, D)
    wpos[TABLE + 2 :, :] = jnp.zeros((wpos.shape[0] - TABLE - 2, D), LOW)

    def take_head(j, carry):
        value = flatg[pl.ds(HEAD_AT + j, GROUPS, stride=GROUP_ROWS), :].astype(LOW)
        whead[:, pl.ds(pl.multiple_of(j * LANES, LANES), LANES)] = value
        return carry

    lax.fori_loop(0, GROUP_ROWS, take_head, 0)
    whead[:, GROUP_ROWS * LANES :] = jnp.zeros((GROUPS, LANES), LOW)
    patch_bias = take_row(flatg, PATCH_BIAS_AT, D)
    final_gain = take_row(flatg, FINAL_GAIN_AT, D)
    final_bias = take_row(flatg, FINAL_BIAS_AT, D)
    head_bias = take_row(flatg, HEAD_BIAS_AT, HEAD_LANES)

    row_at = (
        (PRE_GAIN_AT, D), (PRE_BIAS_AT, D), (QUERY_BIAS_AT, D), (VALUE_BIAS_AT, D), (PROJ_BIAS_AT, D),
        (MID_GAIN_AT, D), (MID_BIAS_AT, D), (FC1_BIAS_AT, FF), (FC2_BIAS_AT, D),
    )

    def take_layer(n, buf):
        spread(buf, flat, LAYER_ROWS)
        take(flat, wqkv.at[n], QKV_AT, D, 3 * D)
        take(flat, wproj.at[n], PROJ_AT, D, D)
        take(flat, wfc1.at[n], FC1_AT, D, FF)
        take(flat, wfc2.at[n], FC2_AT, FF, D)
        for i, (at, width) in enumerate(row_at):
            vecs[n, i : i + 1, :width] = take_row(flat, at, width)

    def vec(n, i):
        return vecs[n, i : i + 1, : row_at[i][1]]

    loads[1].wait()
    take_layer(0, b0)

    def tile_rows(i):
        return pl.ds(pl.multiple_of(i * ROWS, ROWS), ROWS)

    def onehot_of(place):
        iota = lax.broadcasted_iota(jnp.int32, (1, wpos.shape[0]), 1).astype(FULL)
        return (place == iota).astype(LOW)

    def embed(i, carry):
        r = tile_rows(i)
        place = pos_col[r, 0:1]
        pixel = dot(pat[r, :], wpat[...]) + patch_bias
        stream = dot(onehot_of(place), wpos[...]) + jnp.where(place < TABLE, pixel, 0.0)
        x0[r, :] = stream
        unit, inverse = normalise(stream)
        unit_a[r, :] = unit
        inv_a[r, :] = jnp.broadcast_to(inverse, (ROWS, LANES))
        h = (unit * vec(0, 0) + vec(0, 1)).astype(LOW)
        h_a[r, :] = h
        bias = jnp.concatenate([vec(0, 2), jnp.zeros((1, D), FULL), vec(0, 3)], axis=1)
        qkv[r, :] = (dot(h, wqkv[0]) + bias).astype(LOW)
        return carry

    lax.fori_loop(0, SEQ // ROWS, embed, 0)

    def window_rows(j):
        start = jnp.minimum((102 * j) // 16 * 16, SEQ - WINDOW)
        return pl.ds(pl.multiple_of(start, 16), WINDOW)

    def both(x):
        zero = jnp.zeros_like(x)
        return jnp.concatenate([jnp.where(head_of_lane == 0, x, zero), jnp.where(head_of_lane == 1, x, zero)], axis=0)

    def merge(x):
        return jnp.where(head_of_lane == 0, x[:WINDOW], x[WINDOW:])

    att[...] = jnp.zeros_like(att)

    def attend(j, carry):
        r = window_rows(j)
        own = seg_col[r, :]
        other = jnp.transpose(own)
        first = (2 * j).astype(FULL)
        mask = (own == other) & (own >= first) & (own < first + 2.0)
        mask = jnp.concatenate([mask.astype(FULL)] * 2, axis=0) > 0.5
        for g in range(HEADS // 2):
            lanes = slice(g * LANES, (g + 1) * LANES)
            q2 = both(qkv[r, lanes])
            keys = qkv[r, D + g * LANES : D + (g + 1) * LANES]
            values = qkv[r, 2 * D + g * LANES : 2 * D + (g + 1) * LANES]
            scores = jnp.where(mask, dot_nt(q2, keys) * SCORE_SCALE, MASK_FILL)
            e = jnp.exp(scores - jnp.max(scores, axis=-1, keepdims=True))
            p = jnp.where(mask, e / jnp.sum(e, axis=-1, keepdims=True), 0.0)
            probs[j, g] = p
            att[r, lanes] += merge(dot(p.astype(LOW), values))
        return carry

    lax.fori_loop(0, WINDOWS, attend, 0)

    def feed(i, carry):
        r = tile_rows(i)
        attended = att[r, :].astype(LOW)
        attl[r, :] = attended
        middle = x0[r, :] + dot(attended, wproj[0]) + vec(0, 4)
        unit, inverse = normalise(middle)
        unit_b[r, :] = unit
        inv_b[r, :] = jnp.broadcast_to(inverse, (ROWS, LANES))
        h = (unit * vec(0, 5) + vec(0, 6)).astype(LOW)
        h_b[r, :] = h
        for c in range(4):
            lanes = slice(c * D, (c + 1) * D)
            value, slope = gelu_parts(dot(h, wfc1[0, :, lanes]) + vecs[0, 7:8, lanes])
            act[r, lanes] = value.astype(LOW)
            dgelu[r, lanes] = slope
        x1[r, :] = middle + dot(act[r, :], wfc2[0]) + vec(0, 8)
        return carry

    lax.fori_loop(0, SEQ // ROWS, feed, 0)

    loads[2].wait()
    take_layer(1, b1)
    unit_c = x0
    inv_c = att.at[:, 0:LANES]
    h_c = low

    def kv_rows(i, carry):
        r = tile_rows(i)
        unit, inverse = normalise(x1[r, :])
        unit_c[r, :] = unit
        inv_c[r, :] = jnp.broadcast_to(inverse, (ROWS, LANES))
        h = (unit * vec(1, 0) + vec(1, 1)).astype(LOW)
        h_c[r, :] = h
        bias = jnp.concatenate([jnp.zeros((1, D), FULL), vec(1, 3)], axis=1)
        kv[r, :] = (dot(h, wqkv[1, :, D:]) + bias).astype(LOW)
        return carry

    lax.fori_loop(0, SEQ // ROWS, kv_rows, 0)

    h_s = dot(picker_low, h_c[...]).astype(LOW)
    x_s = dot(picker, x1[...], precision=HIGHEST)
    q_s = (dot(h_s, wqkv[1, :, :D]) + vec(1, 2)).astype(LOW)
    stack_rows = lax.broadcasted_iota(jnp.int32, (HEADS * PICKED, 1), 0)
    stack_lanes = lax.broadcasted_iota(jnp.int32, (1, D), 1)
    own_head = (stack_rows // PICKED) == (stack_lanes // HEAD_DIM)

    def stack(x):
        tall = jnp.concatenate([x.astype(FULL)] * HEADS, axis=0)
        return jnp.where(own_head, tall, 0.0).astype(LOW)

    def unstack(x):
        x = jnp.where(own_head, x, 0.0)
        total = x[:PICKED]
        for h in range(1, HEADS):
            total += x[h * PICKED : (h + 1) * PICKED]
        return total

    q6 = stack(q_s)
    image6 = jnp.concatenate([picked_image] * HEADS, axis=0)
    mask6 = image6 == seg_row
    scores = jnp.where(mask6, dot_nt(q6, kv[:, :D]) * SCORE_SCALE, MASK_FILL)
    e = jnp.exp(scores - jnp.max(scores, axis=-1, keepdims=True))
    p6 = e / jnp.sum(e, axis=-1, keepdims=True)
    p6_low = p6.astype(LOW)
    att_s = unstack(dot(p6_low, kv[:, D:])).astype(LOW)
    mid_s = x_s + dot(att_s, wproj[1]) + vec(1, 4)
    unit_m, inv_m = normalise(mid_s)
    h2_s = (unit_m * vec(1, 5) + vec(1, 6)).astype(LOW)
    act_s, slope_s = gelu_parts(dot(h2_s, wfc1[1]) + vec(1, 7))
    act_s = act_s.astype(LOW)
    x2_s = mid_s + dot(act_s, wfc2[1]) + vec(1, 8)

    unit_f, inv_f = normalise(x2_s)
    summary = (unit_f * final_gain + final_bias).astype(LOW)
    arr_row = lax.broadcasted_iota(jnp.int32, (D, GROUP * LANES), 0)
    arr_lane = lax.broadcasted_iota(jnp.int32, (D, GROUP * LANES), 1)
    arrange = (
        (arr_row == (arr_lane % LANES) * GROUP + arr_lane // LANES) & (arr_lane % LANES < GROUPS)
    ).astype(FULL)
    arranged = dot(summary, arrange.astype(LOW)).astype(LOW)
    logits = head_bias
    spans = []
    for k in range(GROUP):
        at = 2 * CLASSES * k
        block, shift = at // LANES, at % LANES
        blocks = (at + 2 * CLASSES - 1) // LANES - block + 1
        spans.append((block, shift, blocks))
        s_k = arranged[:, k * LANES : k * LANES + GROUPS]
        wide = (HEAD_LANES // LANES + 1) * LANES
        part = dot(s_k, whead[:, block * LANES : block * LANES + wide])
        if shift:
            part = pltpu.roll(part, wide - shift, 1)
        logits = logits + part[:, :HEAD_LANES]
    column = lax.broadcasted_iota(jnp.int32, (PICKED, HEAD_LANES), 1)
    second = picked_row >= IMAGES
    low_end = jnp.where(second, CLASSES, 0)
    valid = (column >= low_end) & (column < low_end + CLASSES)
    live = picked_row < 2 * IMAGES
    target = jnp.zeros((PICKED, 1), jnp.int32)
    for i in range(IMAGES):
        target = jnp.where(picked_row == i, lab[0, i], target)
        target = jnp.where(picked_row == IMAGES + i, CLASSES + tea[0, i], target)
    hit = column == target
    logits = jnp.where(valid, logits, -3e38)
    top = jnp.max(logits, axis=-1, keepdims=True)
    e = jnp.exp(logits - top)
    total = jnp.sum(e, axis=-1, keepdims=True)
    hit_logit = jnp.sum(jnp.where(hit, logits, 0.0), axis=-1, keepdims=True)
    each = jnp.where(live, top + jnp.log(total) - hit_logit, 0.0)
    loss[...] = jnp.broadcast_to(jnp.sum(each, axis=0, keepdims=True), loss.shape)
    grad_logits = jnp.where(live, (e / total - hit.astype(FULL)) * loss_scale, 0.0)
    grad_low = grad_logits.astype(LOW)
    grad_wide = jnp.concatenate([grad_low.astype(FULL), jnp.zeros((PICKED, LANES), FULL)], axis=1)

    grad_arranged = []
    for k, (block, shift, blocks) in enumerate(spans):
        turned = (pltpu.roll(grad_wide, shift, 1) if shift else grad_wide).astype(LOW)
        turned = turned[:, : blocks * LANES]
        s_k = arranged[:, k * LANES : k * LANES + GROUPS]
        grad_w = dot_tn(s_k, turned)
        for j in range(blocks):
            rows = pl.ds(HEAD_AT + block + j, GROUPS, stride=GROUP_ROWS)
            piece = grad_w[:, j * LANES : (j + 1) * LANES]
            if k and j == 0:
                piece = piece + flatg[rows, :]
            flatg[rows, :] = piece
        back = dot_nt(turned, whead[:, block * LANES : (block + blocks) * LANES])
        grad_arranged.append(jnp.concatenate([back, jnp.zeros((PICKED, LANES - GROUPS), FULL)], axis=1))
    grad_summary = dot_nt(jnp.concatenate(grad_arranged, axis=1), arrange, HIGHEST)
    put_row(HEAD_BIAS_AT, col_sum(grad_low), flatg)
    put_row(FINAL_GAIN_AT, col_sum(grad_summary * unit_f), flatg)
    put_row(FINAL_BIAS_AT, col_sum(grad_summary), flatg)
    flatg[GLOBAL_END:, :] = jnp.zeros((PARTS * GLOBAL_ROWS - GLOBAL_END, LANES), FULL)
    dx_s = norm_back(grad_summary, final_gain, unit_f, inv_f)

    out_s = dx_s.astype(LOW)
    for c in range(4):
        put(FC2_AT, c * D, D, dot_tn(act_s[:, c * D : (c + 1) * D], out_s))
    put_row(FC2_BIAS_AT, col_sum(out_s))
    gpre_s = (dot_nt(out_s, wfc2[1]) * slope_s).astype(LOW)
    put(FC1_AT, 0, FF, dot_tn(h2_s, gpre_s))
    put_row(FC1_BIAS_AT, col_sum(gpre_s))
    gh2_s = dot_nt(gpre_s, wfc1[1])
    put_row(MID_GAIN_AT, col_sum(gh2_s * unit_m))
    put_row(MID_BIAS_AT, col_sum(gh2_s))
    gmid_s = dx_s + norm_back(gh2_s, vec(1, 5), unit_m, inv_m)
    gmid_low = gmid_s.astype(LOW)
    put(PROJ_AT, 0, D, dot_tn(att_s, gmid_low))
    put_row(PROJ_BIAS_AT, col_sum(gmid_low))
    gatt6 = stack(dot_nt(gmid_low, wproj[1]).astype(LOW))
    gprob = dot_nt(gatt6, kv[:, D:])
    gscore = (p6 * (gprob - jnp.sum(p6 * gprob, axis=-1, keepdims=True))).astype(LOW)
    gq_s = (unstack(dot(gscore, kv[:, :D])) * SCORE_SCALE).astype(LOW)
    gkeys = (dot_tn(gscore, q6) * SCORE_SCALE).astype(LOW)
    gvalues = dot_tn(p6_low, gatt6).astype(LOW)
    put_row(QUERY_BIAS_AT, col_sum(gq_s))
    put_row(VALUE_BIAS_AT, col_sum(gvalues))
    kv[:, :D] = gkeys
    kv[:, D:] = gvalues
    put(QKV_AT, 0, 3 * D, dot_tn(h_s, gq_s))
    put(QKV_AT, 0, 3 * D, dot_tn(h_c[...], kv[:, :D]), 3)
    put(QKV_AT, 0, 3 * D, dot_tn(h_c[...], kv[:, D:]), 6)
    back_s = jnp.concatenate([dot_nt(gq_s, wqkv[1, :, :D]), gmid_s], axis=1)

    dx = x1

    def kv_back(i, carry):
        gain_sum, bias_sum = carry
        r = tile_rows(i)
        image_col = seg_col[r, 0:1]
        place_col = pos_col[r, 0:1]
        lane = lax.broadcasted_iota(jnp.int32, (1, PICKED), 1).astype(FULL)
        lane_image = jnp.where(lane < IMAGES, lane, lane - IMAGES)
        lane_place = jnp.where(lane < IMAGES, float(TABLE), TABLE + 1.0)
        back_pick = (
            (image_col == lane_image) & (place_col == lane_place) & (lane < 2.0 * IMAGES)
        ).astype(FULL)
        back = dot(back_pick, back_s, precision=HIGHEST)
        grad = back[:, :D] + dot_nt(kv[r, :], wqkv[1, :, D:])
        unit = unit_c[r, :]
        dx[r, :] = back[:, D:] + norm_back(grad, vec(1, 0), unit, inv_c[r, 0:1])
        return gain_sum + col_sum(grad * unit), bias_sum + col_sum(grad)

    zero_row = jnp.zeros((1, D), FULL)
    gain_sum, bias_sum = lax.fori_loop(0, SEQ // ROWS, kv_back, (zero_row, zero_row))
    put_row(PRE_GAIN_AT, gain_sum)
    put_row(PRE_BIAS_AT, bias_sum)
    flat[LAYER_END:, :] = jnp.zeros((PARTS * LAYER_ROWS - LAYER_END, LANES), FULL)
    gather_rows(b1, flat, LAYER_ROWS)
    store1 = pltpu.make_async_copy(b1, g1, sems.at[3])
    store1.start()

    def feed_back(i, carry):
        fc1_sum, fc2_sum, proj_sum, gain_sum, bias_sum = carry
        r = tile_rows(i)
        grad_out = dx[r, :]
        out_low = grad_out.astype(LOW)
        low[r, :] = out_low
        for c in range(4):
            lanes = slice(c * D, (c + 1) * D)
            gpre[r, lanes] = (dot_nt(out_low, wfc2[0, lanes, :]) * dgelu[r, lanes]).astype(LOW)
        grad_h = dot_nt(gpre[r, :], wfc1[0])
        unit = unit_b[r, :]
        middle = grad_out + norm_back(grad_h, vec(0, 5), unit, inv_b[r, 0:1])
        dx[r, :] = middle
        middle_low = middle.astype(LOW)
        h2low[r, :] = middle_low
        gatt[r, :] = dot_nt(middle_low, wproj[0]).astype(LOW)
        return (
            fc1_sum + col_sum(gpre[r, :]), fc2_sum + col_sum(out_low), proj_sum + col_sum(middle_low),
            gain_sum + col_sum(grad_h * unit), bias_sum + col_sum(grad_h),
        )

    h2low = kv.at[:, 0:D]
    gatt = kv.at[:, D : 2 * D]
    sums = lax.fori_loop(0, SEQ // ROWS, feed_back, (jnp.zeros((1, FF), FULL),) + (zero_row,) * 4)
    for at, value in zip((FC1_BIAS_AT, FC2_BIAS_AT, PROJ_BIAS_AT, MID_GAIN_AT, MID_BIAS_AT), sums):
        put_row(at, value)

    for c in range(4):
        lanes = slice(c * D, (c + 1) * D)
        put(FC2_AT, c * D, D, dot_tn(act[:, lanes], low[...]))
        put(FC1_AT, 0, FF, dot_tn(h_b[...], gpre[:, lanes]), 3 * c)
    put(PROJ_AT, 0, D, dot_tn(attl[...], h2low[...]))

    dqkv = dgelu.at[:, : 3 * D]
    dqkv[...] = jnp.zeros(dqkv.shape, FULL)

    def attend_back(j, carry):
        r = window_rows(j)
        for g in range(HEADS // 2):
            lanes = slice(g * LANES, (g + 1) * LANES)
            key_lanes = slice(D + g * LANES, D + (g + 1) * LANES)
            value_lanes = slice(2 * D + g * LANES, 2 * D + (g + 1) * LANES)
            q2 = both(qkv[r, lanes])
            go2 = both(gatt[r, lanes])
            p = probs[j, g]
            gp = dot_nt(go2, qkv[r, value_lanes])
            gs = (p * (gp - jnp.sum(p * gp, axis=-1, keepdims=True))).astype(LOW)
            dqkv[r, lanes] += merge(dot(gs, qkv[r, key_lanes]))
            dqkv[r, key_lanes] += dot_tn(gs, q2)
            dqkv[r, value_lanes] += dot_tn(p.astype(LOW), go2)
        return carry

    lax.fori_loop(0, WINDOWS, attend_back, 0)

    def qkv_back(i, carry):
        query_sum, value_sum, gain_sum, bias_sum, embed_sum = carry
        r = tile_rows(i)
        gq = (dqkv[r, :D] * SCORE_SCALE).astype(LOW)
        gk = (dqkv[r, D : 2 * D] * SCORE_SCALE).astype(LOW)
        gv = dqkv[r, 2 * D :].astype(LOW)
        qkv[r, :D] = gq
        qkv[r, D : 2 * D] = gk
        qkv[r, 2 * D :] = gv
        grad = dot_nt(qkv[r, :], wqkv[0])
        unit = unit_a[r, :]
        full = dx[r, :] + norm_back(grad, vec(0, 0), unit, inv_a[r, 0:1])
        dx[r, :] = full
        place = pos_col[r, 0:1]
        pixel = jnp.where(place < TABLE, full, 0.0).astype(LOW)
        low[r, :] = pixel
        return (
            query_sum + col_sum(gq), value_sum + col_sum(gv), gain_sum + col_sum(grad * unit),
            bias_sum + col_sum(grad), embed_sum + col_sum(pixel),
        )

    sums = lax.fori_loop(0, SEQ // ROWS, qkv_back, (zero_row,) * 5)
    for at, value in zip((QUERY_BIAS_AT, VALUE_BIAS_AT, PRE_GAIN_AT, PRE_BIAS_AT), sums):
        put_row(at, value)
    for c in range(3):
        put(QKV_AT, 0, 3 * D, dot_tn(h_a[...], qkv[:, c * D : (c + 1) * D]), 3 * c)
    gather_rows(b0, flat, LAYER_ROWS)
    store0 = pltpu.make_async_copy(b0, g0, sems.at[4])
    store0.start()

    for c in range(2):
        put(PATCH_AT, c * D, D, dot_tn(pat[:, c * D : (c + 1) * D], low[...]), 0, flatg)
    place = pos_col[:, 0:1]
    onehot = onehot_of(place)
    high = dx[...].astype(LOW)
    rest = (dx[...] - high.astype(FULL)).astype(LOW)
    table = dot_tn(onehot, high) + dot_tn(onehot, rest)
    put(POS_AT, 0, D, table[: TABLE + 2], 0, flatg)
    put_row(PATCH_BIAS_AT, sums[4], flatg)
    gather_rows(bg, flatg, GLOBAL_ROWS)
    store1.wait()
    store0.wait()
    last = pltpu.make_async_copy(bg, gg, sems.at[5])
    last.start()
    last.wait()


def step_call(loss_scale, pat, pos, seg, lab, tea, a0, a1, ag):
    vmem = pl.BlockSpec(memory_space=pltpu.VMEM)
    smem = pl.BlockSpec(memory_space=pltpu.SMEM)
    hbm = pl.BlockSpec(memory_space=pl.ANY)
    shape = lambda *dims, kind=FULL: pltpu.VMEM(dims, kind)
    scratch = [
        shape(*a0.shape, kind=LOW), shape(*a1.shape, kind=LOW), shape(*ag.shape, kind=LOW),
        shape(PARTS * LAYER_ROWS, LANES), shape(PARTS * GLOBAL_ROWS, LANES),
        shape(2, D, 3 * D, kind=LOW), shape(2, D, D, kind=LOW), shape(2, D, FF, kind=LOW), shape(2, FF, D, kind=LOW),
        shape(PATCH, D, kind=LOW), shape(256, D, kind=LOW), shape(GROUPS, (GROUP_ROWS + 1) * LANES, kind=LOW),
        shape(2, 16, FF),
        shape(SEQ, LANES), shape(SEQ, LANES),
        shape(SEQ, D), shape(SEQ, LANES), shape(SEQ, D, kind=LOW),
        shape(SEQ, D), shape(SEQ, LANES), shape(SEQ, D, kind=LOW),
        shape(SEQ, 3 * D, kind=LOW), shape(WINDOWS, HEADS // 2, 2 * WINDOW, WINDOW),
        shape(SEQ, D), shape(SEQ, D, kind=LOW), shape(SEQ, D), shape(SEQ, D),
        shape(SEQ, FF), shape(SEQ, FF, kind=LOW), shape(SEQ, FF, kind=LOW),
        shape(SEQ, 2 * D, kind=LOW), shape(SEQ, D, kind=LOW),
        pltpu.SemaphoreType.DMA((6,)),
    ]
    return pl.pallas_call(
        functools.partial(step_kernel, loss_scale),
        out_shape=[jax.ShapeDtypeStruct(a.shape, LOW) for a in (a0, a1, ag)]
        + [jax.ShapeDtypeStruct((8, LANES), FULL)],
        in_specs=[vmem] * 3 + [smem] * 2 + [hbm] * 3,
        out_specs=[hbm] * 3 + [vmem],
        scratch_shapes=scratch,
        compiler_params=pltpu.CompilerParams(vmem_limit_bytes=VMEM_BYTES),
    )(pat, pos, seg, lab, tea, a0, a1, ag)


VMEM_BYTES = 62 * 1024 * 1024


def adam(master, moment, second, gradient, factor):
    clipped = gradient * factor
    new_moment = BETA_ONE * moment + (1.0 - BETA_ONE) * clipped
    new_second = BETA_TWO * second + (1.0 - BETA_TWO) * clipped * clipped
    fix_one = 1.0 - BETA_ONE**STEP
    fix_two = 1.0 - BETA_TWO**STEP
    update = new_moment / fix_one / (jnp.sqrt(new_second / fix_two) + ADAM_EPS) + WEIGHT_DECAY * master
    return master - LEARN_RATE * update, new_moment, new_second


MESH = pl.DeviceIdType.MESH


class Place:
    def __init__(self, sizes):
        dp, fsdp = sizes
        self.ny = dp // 2
        self.nx = next(v for v in range(min(self.ny, fsdp), 0, -1) if fsdp % v == 0)
        self.nz = fsdp // self.nx
        self.fsdp = fsdp
        self.count = dp * fsdp
        self.turn = self.nx == self.ny
        self.np_, self.nq = self.ny, self.nx

    def locate(self):
        dp, fsdp = lax.axis_index("dp"), lax.axis_index("fsdp")
        self.y, self.core = dp // 2, dp % 2
        self.z, self.x = fsdp // self.nx, fsdp % self.nx

    def order(self, dz, dp, dq):
        return (dz * self.np_ + dp) * self.nq + dq

    def at(self, dz, dp, dq, other=0):
        core = (self.core + other) % 2
        z = (self.z + dz) % self.nz
        if self.turn:
            y = jnp.where(core == 0, self.y + dp, self.y + dq) % self.ny
            x = jnp.where(core == 0, self.x + dq, self.x + dp) % self.nx
        else:
            y, x = (self.y + dp) % self.ny, (self.x + dq) % self.nx
        return y * 2 + core, z * self.nx + x

    def piece(self, dz, dp, dq, other=0):
        a, b = self.at(dz, dp, dq, other)
        return a * self.fsdp + b

    def offsets(self):
        return [(a, b, c) for a in range(self.nz) for b in range(self.np_) for c in range(self.nq)]

    def core_at(self, k):
        return self.at(0, 0, 0, k)

    def y_at(self, k):
        return (self.y + k) % self.ny * 2 + self.core, self.z * self.nx + self.x

    def x_at(self, k):
        return self.y * 2 + self.core, self.z * self.nx + (self.x + k) % self.nx

    def peers(self):
        ids = [self.at(0, 0, 0, 1)]
        ids += [self.at(k, 0, 0) for k in range(1, self.nz)]
        ids += [self.at(0, k, 0) for k in range(1, self.np_)]
        ids += [self.at(0, 0, k) for k in range(1, self.nq)]
        return ids

    def greet(self):
        barrier = pltpu.get_barrier_semaphore()
        ids = self.peers()
        for peer in ids:
            pl.semaphore_signal(barrier, inc=1, device_id=peer, device_id_type=MESH)
        pl.semaphore_wait(barrier, len(ids))


def gather_kernel(place, lm, gm, o0, o1, og, own0, own1, owng, send, local, recv):
    place.locate()
    me = place.piece(0, 0, 0)
    chunks = ((og, owng), (o0, own0), (o1, own1))
    owng[: gm.shape[0], :] = gm[...].astype(LOW)
    own0[: lm.shape[1], :] = lm[0].astype(LOW)
    own1[: lm.shape[1], :] = lm[1].astype(LOW)
    place.greet()

    def push(n, src, piece, index, peer):
        out = chunks[n][0]
        pltpu.make_async_remote_copy(
            src_ref=src, dst_ref=out.at[piece], send_sem=send.at[n], recv_sem=recv.at[n, index],
            device_id=peer, device_id_type=MESH,
        ).start()

    def forward(n, d):
        dz, dp, dq = d
        piece = place.piece(*d)
        mine = d == (0, 0, 0)
        src = chunks[n][1] if mine else chunks[n][0].at[piece]
        if mine:
            for k in range(1, place.nz):
                push(n, src, piece, place.order(-k % place.nz, 0, 0), place.at(k, 0, 0))
        if dp == 0 and dq == 0:
            for k in range(1, place.np_):
                push(n, src, piece, place.order(dz, -k % place.np_, 0), place.at(0, k, 0))
        if dq == 0:
            for k in range(1, place.nq):
                push(n, src, piece, place.order(dz, dp, -k % place.nq), place.at(0, 0, k))
        push(n, src, piece, place.count // 2 + place.order(*d), place.at(0, 0, 0, 1))

    def arrive(n, piece, index):
        out = chunks[n][0]
        pltpu.make_async_remote_copy(
            src_ref=out.at[piece], dst_ref=out.at[piece], send_sem=send.at[n], recv_sem=recv.at[n, index],
            device_id=place.at(0, 0, 0, 1), device_id_type=MESH,
        ).wait_recv()

    keeps = []
    for n, (out, own) in enumerate(chunks):
        forward(n, (0, 0, 0))
        keep = pltpu.make_async_copy(own, out.at[me], local.at[n])
        keep.start()
        keeps.append(keep)
    rest = sorted(place.offsets()[1:], key=lambda d: ((d[0] > 0) + 2 * (d[1] > 0) + 4 * (d[2] > 0), d))
    for n in range(3):
        for d in rest:
            arrive(n, place.piece(*d), place.order(*d))
            forward(n, d)
    for n, (out, own) in enumerate(chunks):
        for d in place.offsets():
            arrive(n, place.piece(*d, 1), place.count // 2 + place.order(*d))
        keeps[n].wait()
        sent = out.at[pl.ds(0, place.count - 1)]
        pltpu.make_async_copy(sent, sent, send.at[n]).wait()


def scatter_kernel(
    place, g0, g1, gg, loss, s0, s1, sg, total,
    l0, l1, lg, c0, c1, cg, q0, q1, qg, p0, p1, pg, z0, z1, zg, tiles,
    send, local, recv, tile_send, tile_recv,
):
    place.locate()
    nz, np_, nq = place.nz, place.np_, place.nq
    half = place.count // 2
    chunks = ((g1, l1, c1, q1, p1, z1, s1), (g0, l0, c0, q0, p0, z0, s0), (gg, lg, cg, qg, pg, zg, sg))
    far = sorted(place.offsets(), key=lambda d: (-(d[2] > 0), -(d[1] > 0), -(d[0] > 0), d))
    q_base, p_base, z_base = half, half + nz * np_ * (nq - 1), half + nz * np_ * (nq - 1) + nz * (np_ - 1)

    def push(n, src, dst, index, peer):
        pltpu.make_async_remote_copy(
            src_ref=src, dst_ref=dst, send_sem=send.at[n], recv_sem=recv.at[n, index],
            device_id=peer, device_id_type=MESH,
        ).start()

    def arrive(n, dst, index):
        pltpu.make_async_remote_copy(
            src_ref=dst, dst_ref=dst, send_sem=send.at[n], recv_sem=recv.at[n, index],
            device_id=place.at(0, 0, 0, 1), device_id_type=MESH,
        ).wait_recv()

    loads = {}
    for n, (g, l, *_) in enumerate(chunks):
        for d in far:
            i = place.order(*d)
            loads[n, d] = pltpu.make_async_copy(g.at[place.piece(*d)], l.at[i], local.at[n, i])
            loads[n, d].start()
    place.greet()
    for n, (g, l, c, *_) in enumerate(chunks):
        for d in far:
            i = place.order(*d)
            push(n, g.at[place.piece(*d, 1)], c.at[i], i, place.at(0, 0, 0, 1))

    def gathered(n, d):
        g, l, c, q, p, z, s = chunks[n]
        dz, dp, dq = d
        i = place.order(*d)
        loads[n, d].wait()
        arrive(n, c.at[i], i)
        refs = [l.at[i], c.at[i]]
        if dq == 0:
            for k in range(nq - 1):
                j = (dz * np_ + dp) * (nq - 1) + k
                arrive(n, q.at[j], q_base + j)
                refs.append(q.at[j])
        if dq == 0 and dp == 0:
            for k in range(np_ - 1):
                j = dz * (np_ - 1) + k
                arrive(n, p.at[j], p_base + j)
                refs.append(p.at[j])
        if d == (0, 0, 0):
            for k in range(nz - 1):
                arrive(n, z.at[k], z_base + k)
                refs.append(z.at[k])
        return refs

    def add_up(refs, dst, kind, rows):
        step = 64 if rows % 64 == 0 else 32 if rows % 32 == 0 else 16

        def one(t, carry):
            r = pl.ds(pl.multiple_of(t * step, step), step)
            value = refs[0][r, :].astype(FULL)
            for ref in refs[1:]:
                value += ref[r, :].astype(FULL)
            dst[r, :] = value.astype(kind)
            return carry

        lax.fori_loop(0, rows // step, one, 0)

    def stage_q(n):
        g, l, c, q, p, z, s = chunks[n]
        for d in far:
            dz, dp, dq = d
            if dq:
                refs = gathered(n, d)
                add_up(refs, refs[0], LOW, l.shape[1])
                j = (dz * np_ + dp) * (nq - 1) + (nq - dq) - 1
                push(n, refs[0], q.at[j], q_base + j, place.at(0, 0, dq))

    def stage_p(n):
        g, l, c, q, p, z, s = chunks[n]
        for d in far:
            dz, dp, dq = d
            if dq == 0 and dp:
                refs = gathered(n, d)
                add_up(refs, refs[0], LOW, l.shape[1])
                j = dz * (np_ - 1) + (np_ - dp) - 1
                push(n, refs[0], p.at[j], p_base + j, place.at(0, dp, 0))

    def stage_z(n):
        g, l, c, q, p, z, s = chunks[n]
        for d in far:
            dz, dp, dq = d
            if dq == 0 and dp == 0 and dz:
                refs = gathered(n, d)
                add_up(refs, refs[0], LOW, l.shape[1])
                j = (nz - dz) - 1
                push(n, refs[0], z.at[j], z_base + j, place.at(dz, 0, 0))

    def stage_own(n):
        g, l, c, q, p, z, s = chunks[n]
        add_up(gathered(n, (0, 0, 0)), s, FULL, l.shape[1])

    stages = (stage_q, stage_p, stage_z, stage_own)
    for t in range(3 + len(stages) - 1):
        for n in range(3):
            if 0 <= t - n < len(stages):
                stages[t - n](n)

    squares = jnp.zeros((1, 1), FULL)
    for s, rows in ((s0, place.rows[0]), (s1, place.rows[0]), (sg, place.rows[1])):
        used = s[:rows, :]
        squares += jnp.sum(jnp.sum(used * used, axis=0, keepdims=True), axis=1, keepdims=True)
    row = lax.broadcasted_iota(jnp.int32, (8, LANES), 0)
    tile = jnp.where(row == 0, squares, loss[...])
    base = 0
    axes = (
        (2, place.core, lambda k: place.core_at(k)), (place.ny, place.y, lambda k: place.y_at(k)),
        (place.nx, place.x, lambda k: place.x_at(k)), (nz, place.z, lambda k: place.at(k, 0, 0)),
    )
    sends = []
    for size, own, peer_at in axes:
        tiles[base + own] = tile
        for k in range(1, size):
            copy = pltpu.make_async_remote_copy(
                src_ref=tiles.at[base + own], dst_ref=tiles.at[base + own], send_sem=tile_send.at[base + k],
                recv_sem=tile_recv.at[base + (size - k)], device_id=peer_at(k), device_id_type=MESH,
            )
            copy.start()
            sends.append(copy)
        for k in range(1, size):
            slot = tiles.at[base + (own + k) % size]
            pltpu.make_async_remote_copy(
                src_ref=slot, dst_ref=slot, send_sem=tile_send.at[base + k], recv_sem=tile_recv.at[base + k],
                device_id=peer_at(k), device_id_type=MESH,
            ).wait_recv()
        tile = tiles[base]
        for k in range(1, size):
            tile += tiles[base + k]
        base += size
    total[...] = tile
    for copy in sends:
        copy.wait_send()
    for n, (g, *_) in enumerate(chunks):
        sent = g.at[pl.ds(0, place.count - 1)]
        pltpu.make_async_copy(sent, sent, send.at[n]).wait()


def padded(rows):
    return rows + -rows % 16


def gather_call(place, lm, gm):
    n, rows, global_rows = place.count, lm.shape[1], gm.shape[0]
    vmem = pl.BlockSpec(memory_space=pltpu.VMEM)
    hbm = pl.BlockSpec(memory_space=pl.ANY)
    shapes = [(padded(rows), LANES), (padded(rows), LANES), (padded(global_rows), LANES)]
    return pl.pallas_call(
        functools.partial(gather_kernel, place),
        out_shape=[jax.ShapeDtypeStruct((n,) + s, LOW) for s in shapes],
        in_specs=[vmem] * 2,
        out_specs=[hbm] * 3,
        scratch_shapes=[pltpu.VMEM(s, LOW) for s in shapes]
        + [
            pltpu.SemaphoreType.DMA((3,)), pltpu.SemaphoreType.DMA((3,)), pltpu.SemaphoreType.DMA((3, n)),
        ],
        compiler_params=pltpu.CompilerParams(collective_id=0, has_side_effects=True, vmem_limit_bytes=VMEM_BYTES),
    )(lm, gm)


def scatter_call(place, g0, g1, gg, loss):
    n = place.count
    vmem = pl.BlockSpec(memory_space=pltpu.VMEM)
    hbm = pl.BlockSpec(memory_space=pl.ANY)
    blocks = [g.shape[1:] for g in (g0, g1, gg)]
    counts = (
        n // 2, n // 2, place.nz * place.np_ * (place.nq - 1), place.nz * (place.np_ - 1), place.nz - 1
    )
    tiles = 2 + place.ny + place.nx + place.nz
    received = n // 2 + sum(counts[2:])
    return pl.pallas_call(
        functools.partial(scatter_kernel, place),
        out_shape=[jax.ShapeDtypeStruct(b, FULL) for b in blocks] + [jax.ShapeDtypeStruct((8, LANES), FULL)],
        in_specs=[hbm] * 3 + [vmem],
        out_specs=[vmem] * 4,
        scratch_shapes=[pltpu.VMEM((max(c, 1),) + b, LOW) for c in counts for b in blocks]
        + [
            pltpu.VMEM((tiles, 8, LANES), FULL),
            pltpu.SemaphoreType.DMA((3,)), pltpu.SemaphoreType.DMA((3, n // 2)),
            pltpu.SemaphoreType.DMA((3, received)),
            pltpu.SemaphoreType.DMA((tiles,)), pltpu.SemaphoreType.DMA((tiles,)),
        ],
        compiler_params=pltpu.CompilerParams(collective_id=1, has_side_effects=True, vmem_limit_bytes=VMEM_BYTES),
    )(g0, g1, gg, loss)


def repack(a, count, rows, new_count, new_rows):
    if (count, rows) == (new_count, new_rows):
        return a
    a = a[:, :rows].reshape(new_count, new_rows, LANES)
    return jnp.pad(a, ((0, 0), (0, padded(new_rows) - new_rows), (0, 0)))


def shards(sizes, pat, pos, seg, lab, tea, lm, lo, ls, gm, go, gs):
    place = Place(sizes)
    n = place.count
    rows, global_rows = lm.shape[1] // LANES, gm.shape[0] // LANES
    place.rows = rows, global_rows
    gathered = gather_call(place, lm.reshape(2, rows, LANES), gm.reshape(global_rows, LANES))
    own_rows = (rows, rows, global_rows)
    step_rows = (LAYER_ROWS, LAYER_ROWS, GLOBAL_ROWS)
    gathered = [repack(a, n, r, PARTS, t) for a, r, t in zip(gathered, own_rows, step_rows)]
    loss_scale = 1.0 / (2 * IMAGES * n)
    *grads, loss = step_call(loss_scale, pat[0], pos, seg, lab, tea, *gathered)
    grads = [repack(a, PARTS, t, n, r) for a, r, t in zip(grads, own_rows, step_rows)]
    s0, s1, sg, total = scatter_call(place, *grads, loss)
    layer = jnp.stack([s0[:rows].reshape(-1), s1[:rows].reshape(-1)])
    gg = sg[:global_rows].reshape(-1)
    norm = jnp.sqrt(total[0, 0])
    factor = jnp.minimum(1.0, CLIP_NORM / norm)
    return adam(lm, lo, ls, layer, factor) + adam(gm, go, gs, gg, factor) + (norm, total[1, 0])


def solution(mesh):
    axes = tuple(mesh.axis_names)
    split = P(axes)
    wide = P(None, axes)
    return jax.shard_map(
        functools.partial(shards, tuple(mesh.shape[a] for a in axes)),
        mesh=mesh,
        in_specs=(split,) * 5 + (wide,) * 3 + (split,) * 3,
        out_specs=(wide,) * 3 + (split,) * 3 + (P(), P()),
        check_vma=False,
    )
```

profile of v0, /device:TPU:0, one launch (start us, length us, event | category | flops | bytes accessed | tf_op | source)
XLA Modules:
  0.0 201.4 jit_solution(10009517868335671229)
XLA Ops:
  0.6 1.8 copy.21
  2.4 58.4 %shard_map.170 = (bf16[32,448,128]{2,1,0:T(8,128)(2,1)}, bf16[32,448,128]{2,1,0:T(8,128)(2,1)}, bf16[32,288,128]{2,1,0:T(8,128)(2,1)}) custom-call(f32[2,440,128]{2,1,0:T(8,128)} %bitcast.17, f32[280,128]{1,0:T(8,128)} %bitcast.22), custom_call_target="tpu_custom_call" | custom-call | tf_op jit(solution)/shard_map/pallas_call | solution.py:875
  60.9 66.3 %shard_map.171 = (bf16[32,448,128]{2,1,0:T(8,128)(2,1)}, bf16[32,448,128]{2,1,0:T(8,128)(2,1)}, bf16[32,288,128]{2,1,0:T(8,128)(2,1)}, f32[8,128]{1,0:T(8,128)}) custom-call(bf16[768,768]{1,0:T(8,128)(2,1)} %bitcast.19, s32[1,768]{1,0:T(1,128)} %pos.1, s32[1,768]{1,0:T(1,128)} %seg.1, s32[1,15]{1,0:T(1,128)} %lab.1, s32[1,15]{1,0:T(1,128)} %tea.1, ...), custom_call_target="tpu_custom_call" | custom-call | tf_op jit(solution)/shard_map/pallas_call | solution.py:570
  127.1 0.0 copy-start.1
  127.2 0.0 copy-start.4
  127.2 0.0 copy-start.5
  127.2 0.0 copy-start
  127.2 0.0 copy-start.2
  127.2 0.0 copy-start.3
  127.2 64.5 %shard_map.172 = (f32[448,128]{1,0:T(8,128)}, f32[448,128]{1,0:T(8,128)}, f32[288,128]{1,0:T(8,128)}, f32[8,128]{1,0:T(8,128)}) custom-call(bf16[32,448,128]{2,1,0:T(8,128)(2,1)} %get-tuple-element.22.g0, bf16[32,448,128]{2,1,0:T(8,128)(2,1)} %get-tuple-element.23.g1, bf16[32,288,128]{2,1,0:T(8,128)(2,1)} %get-tuple-element.24.gg, ...), custom_call_target="tpu_custom_call" | custom-call | tf_op jit(solution)/shard_map/pallas_call | solution.py:898
  191.7 1.0 slice.15
  192.7 1.3 fusion.6
  194.7 1.0 slice.16
  195.7 0.0 copy-done.1
  195.7 0.0 copy-done.4
  195.7 0.0 copy-done.5
  195.7 1.7 multiply_subtract_fusion.1
  197.4 0.0 copy-done
  197.4 0.0 copy-done.2
  197.4 0.0 copy-done.3
  197.5 2.8 %multiply_subtract_fusion = (f32[2,56320]{1,0:T(2,128)}, f32[2,56320]{1,0:T(2,128)}, f32[2,56320]{1,0:T(2,128)}) fusion(f32[2,56320]{1,0:T(2,128)S(1)} %copy-done, f32[]{:T(128)S(6)} %min_shard_map.3, f32[1,56320]{1,0:T(1,128)S(1)} %bitcast.21, f32[1,56320]{1,0:T(1,128)S(1)} %bitcast.20, f32[2,56320]{1,0:T(2,128)S(1)} %copy-done.2, f32[2,56320]{1,0:T(2,128)S(1)} %copy-done.3), kind=kLoop, calls=%fused_computation.4 | loop fusion | flops 1914880 | bytes 3153924 | tf_op jit(solution)/shard_map/sub | solution.py:591
Async XLA Ops:
  127.1 68.5 %copy-start.1 = (f32[35840]{0:T(1024)S(1)}, f32[35840]{0:T(1024)}, u32[]{:S(2)}) copy-start(f32[35840]{0:T(1024)} %param.19) | copy-start | bytes 430084
  127.2 68.5 %copy-start.4 = (f32[35840]{0:T(1024)S(1)}, f32[35840]{0:T(1024)}, u32[]{:S(2)}) copy-start(f32[35840]{0:T(1024)} %param.20) | copy-start | bytes 430084
  127.2 68.5 %copy-start.5 = (f32[35840]{0:T(1024)S(1)}, f32[35840]{0:T(1024)}, u32[]{:S(2)}) copy-start(f32[35840]{0:T(1024)} %param.21) | copy-start | bytes 430084
  127.2 70.3 %copy-start = (f32[2,56320]{1,0:T(2,128)S(1)}, f32[2,56320]{1,0:T(2,128)}, u32[]{:S(2)}) copy-start(f32[2,56320]{1,0:T(2,128)} %param.16) | copy-start | bytes 1351684
  127.2 70.3 %copy-start.2 = (f32[2,56320]{1,0:T(2,128)S(1)}, f32[2,56320]{1,0:T(2,128)}, u32[]{:S(2)}) copy-start(f32[2,56320]{1,0:T(2,128)} %param.17) | copy-start | bytes 1351684
  127.2 70.3 %copy-start.3 = (f32[2,56320]{1,0:T(2,128)S(1)}, f32[2,56320]{1,0:T(2,128)}, u32[]{:S(2)}) copy-start(f32[2,56320]{1,0:T(2,128)} %param.18) | copy-start | bytes 1351684
where the time goes:
time: 202 us; the launch traced here: 201 us
  Pallas kernels  189 us (94%)
  local copies, waits for them, and re-layouts  5.04 us (2%)
  other arithmetic  4.56 us (2%)
  between operations  2.6 us (1%)
    pallas_call x1, Pallas kernels, step_call(): pl.pallas_call(functools.partial(step_kernel, loss_scale), out_shape=[jax...  66.3 us
    pallas_call x1, Pallas kernels, scatter_call(): pl.pallas_call(functools.partial(scatter_kernel, place), out_shape=[jax.S...  64.5 us
    pallas_call x1, Pallas kernels, gather_call(): pl.pallas_call(functools.partial(gather_kernel, place), out_shape=[jax.Sh...  58.4 us
    sub x2, other arithmetic, adam(): return (master - LEARN_RATE * update, new_moment, new_second)  4.56 us

commit v1 on v0

v1 whole, which is shorter than its diff:
```python
import functools

import jax
import jax.numpy as jnp
from jax import lax
from jax.experimental import pallas as pl
from jax.experimental.pallas import tpu as pltpu
from jax.sharding import PartitionSpec as P

D = 384
HEADS = 6
HEAD_DIM = 64
FF = 1536
CLASSES = 1000
PATCH = 768
TABLE = 196
IMAGES = 15
SEQ = 768
STEP = 10
LANES = 128

NORM_EPS = 1e-06
BETA_ONE = 0.9
BETA_TWO = 0.999
ADAM_EPS = 1e-08
LEARN_RATE = 0.1
WEIGHT_DECAY = 0.05
CLIP_NORM = 0.01
MASK_FILL = -1000000000.0
SCORE_SCALE = HEAD_DIM ** (-0.5)
LOW = jnp.bfloat16
FULL = jnp.float32
HIGHEST = lax.Precision.HIGHEST

QKV_AT, PROJ_AT, FC1_AT, FC2_AT = 0, 3456, 4608, 9216
PRE_GAIN_AT, PRE_BIAS_AT, QUERY_BIAS_AT, VALUE_BIAS_AT = 13824, 13827, 13830, 13833
PROJ_BIAS_AT, MID_GAIN_AT, MID_BIAS_AT, FC1_BIAS_AT, FC2_BIAS_AT = 13836, 13839, 13842, 13845, 13857
LAYER_END = 13860
PATCH_AT, POS_AT, PATCH_BIAS_AT, FINAL_GAIN_AT, FINAL_BIAS_AT = 0, 2304, 2898, 2901, 2904
HEAD_AT, HEAD_BIAS_AT, GLOBAL_END = 2907, 8907, 8923
GROUP, GROUP_ROWS, GROUPS = 8, 125, 48
HEAD_LANES = 2048
PICKED = 32
WINDOWS, WINDOW = 8, 128
ROWS = 256
LAYER_ALL, GLOBAL_ALL = 14080, 8960
VMEM_BYTES = 64 * 1024 * 1024 - 64 * 1024
MESH = pl.DeviceIdType.MESH


def dot(a, b, dims=(1, 0), precision=None):
    return lax.dot_general(
        a, b, (((dims[0],), (dims[1],)), ((), ())), precision=precision, preferred_element_type=FULL
    )


def dot_nt(a, b, precision=None):
    return dot(a, b, (1, 1), precision)


def dot_tn(a, b, precision=None):
    return dot(a, b, (0, 0), precision)


def row_mean(x):
    return jnp.sum(x, axis=-1, keepdims=True) * (1.0 / D)


def normalise(x):
    center = x - row_mean(x)
    inverse = lax.rsqrt(row_mean(center * center) + NORM_EPS)
    return center * inverse, inverse


def norm_back(grad, gain, unit, inverse):
    scaled = grad * gain
    return inverse * (scaled - row_mean(scaled) - unit * row_mean(scaled * unit))


def col_sum(x):
    return jnp.sum(x.astype(FULL), axis=0, keepdims=True)


def gelu_parts(x):
    size = jnp.abs(x)
    bell = jnp.exp(-0.5 * x * x)
    base = 1.0 + (0.3275911 * 0.7071067811865476) * size
    t = pl.reciprocal(base, approx=True)
    t = t * (2.0 - base * t)
    tail = ((((1.061405429 * t - 1.453152027) * t + 1.421413741) * t - 0.284496736) * t + 0.254829592) * t
    tail = 0.5 * tail * bell
    phi = jnp.where(x < 0, tail, 1.0 - tail)
    return x * phi, phi + x * (bell * 0.3989422804014327)


def exact_parts(x):
    high = x.astype(LOW)
    rest = x - high.astype(FULL)
    middle = rest.astype(LOW)
    return high, middle, (rest - middle.astype(FULL)).astype(LOW)


def wrap(value, size):
    return jnp.where(value >= size, value - size, value)


class Place:
    def __init__(self, sizes):
        dp, fsdp = sizes
        self.n = self.ny = self.nx = dp // 2
        self.nz = fsdp // self.nx
        assert dp == 2 * self.n and fsdp == self.n * self.nz

    def locate(self):
        dp, fsdp = lax.axis_index("dp"), lax.axis_index("fsdp")
        self.y, self.core = dp // 2, dp % 2
        self.z, self.x = fsdp // self.nx, fsdp % self.nx
        self.even = self.core == 0
        self.zs = [wrap(self.z + k, self.nz) for k in range(self.nz)]
        self.ys = [wrap(self.y + k, self.n) for k in range(self.n)]
        self.xs = [wrap(self.x + k, self.n) for k in range(self.n)]
        spans = [(p, q) for p in range(self.n) for q in range(self.n)]
        self.short = {
            (p, q): (jnp.where(self.even, self.ys[p], self.ys[q]), jnp.where(self.even, self.xs[q], self.xs[p]))
            for p, q in spans
        }

    def yx(self, p, q):
        return self.short[p, q]

    def block(self, dz, p, q):
        y, x = self.yx(p, q)
        return y, self.core, self.zs[dz], x

    def device(self, y, core, z, x):
        return y * 2 + core, z * self.nx + x

    def meet(self):
        self.other = self.device(self.y, 1 - self.core, self.z, self.x)
        self.zp = [self.device(self.y, self.core, z, self.x) for z in self.zs]
        self.yp = [self.device(y, self.core, self.z, self.x) for y in self.ys]
        self.xp = [self.device(self.y, self.core, self.z, x) for x in self.xs]
        self.pp = [self.device(*self.block(0, k, 0)) for k in range(self.n)]
        self.qp = [self.device(*self.block(0, 0, k)) for k in range(self.n)]
        barrier = pltpu.get_barrier_semaphore()
        ids = [self.other] + self.zp[1:] + self.yp[1:] + self.xp[1:]
        for peer in ids:
            pl.semaphore_signal(barrier, inc=1, device_id=peer, device_id_type=MESH)
        pl.semaphore_wait(barrier, len(ids))


def push(src, dst, send, recv, peer):
    pltpu.make_async_remote_copy(
        src_ref=src, dst_ref=dst, send_sem=send, recv_sem=recv, device_id=peer, device_id_type=MESH
    ).start()


def landed(dst, recv):
    pltpu.make_async_copy(dst, dst, recv).wait()


class Gather:
    def __init__(self, place, buf, send, recv):
        self.place, self.buf, self.send, self.recv = place, buf, send, recv
        self.from_p = place.nz
        self.from_q = self.from_p + place.nz * place.n
        self.from_core = self.from_q + place.n

    def to_p(self, dz):
        a, t = self.place, self.buf.at[self.place.block(dz, 0, 0)]
        for k in range(1, a.n):
            push(t, t, self.send, self.recv.at[self.from_p + dz * a.n + a.n - k], a.pp[k])

    def to_q(self, dz, p):
        a, t = self.place, self.buf.at[self.place.block(dz, p, 0)]
        for k in range(1, a.n):
            push(t, t, self.send, self.recv.at[self.from_q + a.n - k], a.qp[k])

    def start(self):
        a, t = self.place, self.buf.at[self.place.block(0, 0, 0)]
        self.to_p(0)
        for k in range(1, a.nz):
            push(t, t, self.send, self.recv.at[a.nz - k], a.zp[k])
        self.to_q(0, 0)

    def z_came(self, dz):
        landed(self.buf.at[self.place.block(dz, 0, 0)], self.recv.at[dz])
        self.to_p(dz)
        self.to_q(dz, 0)

    def p_came(self, dz, p):
        landed(self.buf.at[self.place.block(dz, p, 0)], self.recv.at[self.from_p + dz * self.place.n + p])
        self.to_q(dz, p)

    def group(self, core, q):
        a = self.place
        return self.buf.at[:, 0, :, a.xs[q]] if core == 0 else self.buf.at[a.ys[q], 1]

    def to_core(self, q):
        a = self.place
        for core in range(2):

            @pl.when(a.core == core)
            def _():
                t = self.group(core, q)
                push(t, t, self.send, self.recv.at[self.from_core + q], a.other)

    def q_came(self, q):
        landed(self.buf.at[:, 0, :, 0], self.recv.at[self.from_q + q])
        self.to_core(q)

    def steps(self):
        a = self.place
        near = sorted(range(1, a.nz), key=lambda k: min(k, a.nz - k))
        out = [lambda p=p: self.p_came(0, p) for p in range(1, a.n)]
        out += [lambda k=k: self.z_came(k) for k in near]
        out += [lambda k=k, p=p: self.p_came(k, p) for k in near for p in range(1, a.n)]
        out += [lambda: self.to_core(0)]
        return out

    def last(self):
        for q in range(1, self.place.n):
            self.q_came(q)

    def finish(self):
        for q in range(self.place.n):
            landed(self.buf.at[:, 0, :, 0], self.recv.at[self.from_core + q])

    def drain(self):
        a = self.place
        for t in (self.buf.at[:, 0], self.buf.at[:, 0, :, pl.ds(0, a.n - 1)], self.buf.at[0, 0, :, pl.ds(0, a.n - 1)]):
            landed(t, self.send)
        landed(self.buf.at[0, 0, pl.ds(0, a.nz - 1), 0], self.send)


class Scatter:
    def __init__(self, place, buf, from_core, from_q, from_p, from_z, out, send, recv):
        self.place, self.buf, self.out, self.send, self.recv = place, buf, out, send, recv
        self.core_buf, self.q_buf, self.p_buf, self.z_buf = from_core, from_q, from_p, from_z
        n, nz = place.n, place.nz
        self.at_q = n
        self.at_p = self.at_q + n * n
        self.at_z = self.at_p + n

    def start(self):
        a = self.place
        for core in range(2):

            @pl.when(a.core == core)
            def _():
                for q in tuple(range(1, a.n)) + (0,):
                    if core == 1:
                        src, dst = self.buf.at[:, 0, :, a.xs[q]], self.core_buf.at[:, :, a.xs[q]]
                    else:
                        src, dst = self.buf.at[a.ys[q], 1], self.core_buf.at[a.ys[q]]
                    push(src, dst, self.send, self.recv.at[q], a.other)

    def core_came(self, q):
        landed(self.core_buf.at[0], self.recv.at[q])

    def add(self, p, q, z, extra):
        a = self.place
        y, x = a.yx(p, q)
        mine, theirs = self.buf.at[y, a.core, z, x], self.core_buf.at[y, z, x]
        add_up([mine, theirs] + [ref.at[z] for ref in extra], mine, LOW)

    def q_extra(self, p):
        return [self.q_buf.at[k, p] for k in range(self.place.n - 1)]

    def p_extra(self):
        return [self.p_buf.at[k] for k in range(self.place.n - 1)]

    def to_q(self, p, q):
        a = self.place

        def one(z, carry):
            self.add(p, q, z, [])
            return carry

        lax.fori_loop(0, a.nz, one, 0)
        y, x = a.yx(p, q)
        push(self.buf.at[y, a.core, :, x], self.q_buf.at[a.n - q - 1, p], self.send,
             self.recv.at[self.at_q + (a.n - q) * a.n + p], a.qp[q])

    def q_came(self, p):
        a = self.place
        for k in range(1, a.n):
            landed(self.q_buf.at[k - 1, p], self.recv.at[self.at_q + k * a.n + p])

    def to_p(self, p):
        a = self.place
        self.q_came(p)

        def one(z, carry):
            self.add(p, 0, z, self.q_extra(p))
            return carry

        lax.fori_loop(0, a.nz, one, 0)
        y, x = a.yx(p, 0)
        push(self.buf.at[y, a.core, :, x], self.p_buf.at[a.n - p - 1], self.send, self.recv.at[self.at_p + a.n - p], a.pp[p])

    def p_came(self):
        a = self.place
        self.q_came(0)
        for k in range(1, a.n):
            landed(self.p_buf.at[k - 1], self.recv.at[self.at_p + k])

    def to_z(self, k):
        a = self.place
        self.add(0, 0, a.zs[k], self.q_extra(0) + self.p_extra())
        t = self.buf.at[a.block(k, 0, 0)]
        push(t, self.z_buf.at[a.nz - k - 1], self.send, self.recv.at[self.at_z + a.nz - k], a.zp[k])

    def own(self):
        a = self.place
        for k in range(1, a.nz):
            landed(self.z_buf.at[k - 1], self.recv.at[self.at_z + k])
        mine, theirs = self.buf.at[a.block(0, 0, 0)], self.core_buf.at[a.y, a.z, a.x]
        extra = [ref.at[a.z] for ref in self.q_extra(0) + self.p_extra()]
        add_up([mine, theirs] + extra + [self.z_buf.at[k] for k in range(a.nz - 1)], self.out, FULL)

    def steps(self):
        a = self.place
        out = [self.start]
        for q in range(1, a.n):
            out.append(lambda q=q: self.core_came(q))
            for p in tuple(range(1, a.n)) + (0,):
                out.append(lambda p=p, q=q: self.to_q(p, q))
        out.append(lambda: self.core_came(0))
        for p in range(1, a.n):
            out.append(lambda p=p: self.to_p(p))
        out.append(self.p_came)
        for k in sorted(range(1, a.nz), key=lambda k: -min(k, a.nz - k)):
            out.append(lambda k=k: self.to_z(k))
        out.append(self.own)
        return out

    def drain(self):
        a = self.place
        landed(self.buf.at[:, 0], self.send)
        for _ in range(1, a.n):
            landed(self.buf.at[0, 0], self.send)
            landed(self.buf.at[0, 0, :, 0], self.send)
        landed(self.buf.at[0, 0, pl.ds(0, a.nz - 1), 0], self.send)


def add_up(refs, dst, kind):
    rows = dst.shape[0]
    step = next(v for v in (224, 144, 64, 48, 32, 16) if rows % v == 0)

    def one(t, carry):
        r = pl.ds(pl.multiple_of(t * step, step), step)
        value = refs[0][r, :].astype(FULL)
        for ref in refs[1:]:
            value += ref[r, :].astype(FULL)
        dst[r, :] = value.astype(kind)
        return carry

    lax.fori_loop(0, rows // step, one, 0)


def add_over_slice(place, tile, tiles, send, recv):
    axes = (
        (2, place.core, (None, place.other)), (place.n, place.y, place.yp), (place.n, place.x, place.xp),
        (place.nz, place.z, place.zp),
    )
    base = 0
    for size, own, peers in axes:
        mine = tiles.at[base + own]
        mine[...] = tile
        for k in range(1, size):
            push(mine, mine, send.at[base + k], recv.at[base + size - k], peers[k])
        for k in range(1, size):
            landed(tiles.at[base + wrap(own + k, size)], recv.at[base + k])
        tile = tiles[base]
        for k in range(1, size):
            tile += tiles[base + k]
        for k in range(1, size):
            landed(mine, send.at[base + k])
        base += size
    return tile


def step_kernel(
    place, loss_scale,
    pat, pos, seg, lab, tea, lm, gm,
    s0, s1, sg, shared,
    b0, b1, bg, r0c, r0q, r0p, r0z, r1c, r1q, r1p, r1z, rgc, rgq, rgp, rgz, flat, edge, stage, arrange,
    wqkv, wproj, wfc1, wfc2, wpat, wpos, whead, vecs,
    pos_col, seg_col, unit_a, inv_a, h_a, unit_b, inv_b, h_b, qkv, probs, attl, x0, x1, slope, act, kv, low, inv_c,
    tiles, sends, gather_recv, scatter_recv, tile_send, tile_recv,
):
    layer_rows, global_rows = lm.shape[1], gm.shape[0]
    place.locate()
    me = place.block(0, 0, 0)
    bg[me + (pl.ds(0, global_rows),)] = gm[...].astype(LOW)
    b0[me + (pl.ds(0, layer_rows),)] = lm[0].astype(LOW)
    b1[me + (pl.ds(0, layer_rows),)] = lm[1].astype(LOW)
    place.meet()
    gathers = [Gather(place, buf, sends.at[i], gather_recv.at[i]) for i, buf in enumerate((bg, b0, b1))]
    gather_g, gather_0, gather_1 = gathers
    for gather in gathers:
        gather.start()
    queue = []

    def pump(count=1):
        for _ in range(min(count, len(queue))):
            queue.pop(0)()

    head_of_lane = lax.broadcasted_iota(jnp.int32, (1, LANES), 1) // HEAD_DIM

    def each_block(low_end, high_end, one):
        def body(s, carry):
            x = lax.rem(s, place.nx)
            rest = lax.div(s, place.nx)
            z, rest = lax.rem(rest, place.nz), lax.div(rest, place.nz)
            one(s, (lax.div(rest, 2), lax.rem(rest, 2), z, x))
            return carry

        lax.fori_loop(low_end, high_end, body, 0)

    def spread(buf, rows, low_end=0, high_end=2 * place.n * place.n * place.nz):
        def one(s, t):
            if rows % 8 == 0:
                flat[pl.ds(pl.multiple_of(s * rows, 8), rows), :] = buf[t + (pl.ds(0, rows),)].astype(FULL)
            else:
                stage[: buf.shape[4], :] = buf[t].astype(FULL)

                def row(i, carry):
                    flat[pl.ds(s * rows + i, 1), :] = stage[pl.ds(i, 1), :]
                    return carry

                lax.fori_loop(0, rows, row, 0)

        each_block(low_end, high_end, one)

    def gather_rows(buf, rows, low_end=0, high_end=2 * place.n * place.n * place.nz):
        def one(s, t):
            if rows % 8 == 0:
                buf[t + (pl.ds(0, rows),)] = flat[pl.ds(pl.multiple_of(s * rows, 8), rows), :].astype(LOW)
            else:

                def row(i, carry):
                    stage[pl.ds(i, 1), :] = flat[pl.ds(s * rows + i, 1), :]
                    return carry

                lax.fori_loop(0, rows, row, 0)
                buf[t] = stage[: buf.shape[4], :].astype(LOW)

        each_block(low_end, high_end, one)

    def take(dst, at, rows, width):
        count = width // LANES

        def one(c, carry):
            value = flat[pl.ds(at + c, rows, stride=count), :].astype(LOW)
            dst[:rows, pl.ds(pl.multiple_of(c * LANES, LANES), LANES)] = value
            return carry

        lax.fori_loop(0, count, one, 0)

    def take_row(at, width):
        return jnp.concatenate([flat[at + i : at + i + 1, :] for i in range(width // LANES)], axis=1)

    def put_row(at, value):
        for i in range(value.shape[1] // LANES):
            flat[at + i : at + i + 1, :] = value[:, i * LANES : (i + 1) * LANES]

    def put(at, start, width, value, first=0):
        count = width // LANES
        rows = value.shape[0]
        for i in range(value.shape[1] // LANES):
            flat[pl.ds(at + start * count + first + i, rows, stride=count), :] = value[:, i * LANES : (i + 1) * LANES]

    for i in range(SEQ // LANES):
        lanes = slice(i * LANES, (i + 1) * LANES)
        for src, dst in ((pos, pos_col), (seg, seg_col)):
            dst[lanes, :] = jnp.transpose(jnp.broadcast_to(src[0:1, lanes].astype(FULL), (LANES, LANES)))
    pos_row = pos[0:1, :]
    seg_row = seg[0:1, :]
    picked_row = lax.broadcasted_iota(jnp.int32, (PICKED, 1), 0)
    picked_image = jnp.where(picked_row < IMAGES, picked_row, picked_row - IMAGES)
    picked_image = jnp.where(picked_row < 2 * IMAGES, picked_image, -1)
    picked_place = jnp.where(picked_row < IMAGES, TABLE, TABLE + 1)
    picker = ((seg_row == picked_image) & (pos_row == picked_place)).astype(FULL)
    picker_low = picker.astype(LOW)

    arr_row = lax.broadcasted_iota(jnp.int32, (D, GROUP * LANES), 0)
    arr_lane = lax.broadcasted_iota(jnp.int32, (D, GROUP * LANES), 1)
    arrange[...] = (
        (arr_row == (arr_lane % LANES) * GROUP + arr_lane // LANES) & (arr_lane % LANES < GROUPS)
    ).astype(FULL).astype(LOW)

    queue.extend(gather_g.steps())
    pump(99)
    queue.extend(gather_0.steps())
    pump(4)
    gather_g.last()
    gather_g.finish()
    spread(bg, global_rows)
    pump(99)
    take(wpat, PATCH_AT, PATCH, D)
    take(wpos, POS_AT, TABLE + 2, D)
    wpos[TABLE + 2 :, :] = jnp.zeros((wpos.shape[0] - TABLE - 2, D), LOW)

    def take_head(j, carry):
        value = flat[pl.ds(HEAD_AT + j, GROUPS, stride=GROUP_ROWS), :].astype(LOW)
        whead[:, pl.ds(pl.multiple_of(j * LANES, LANES), LANES)] = value
        return carry

    lax.fori_loop(0, GROUP_ROWS, take_head, 0)
    whead[:, GROUP_ROWS * LANES :] = jnp.zeros((GROUPS, LANES), LOW)
    patch_bias = take_row(PATCH_BIAS_AT, D)
    final_gain = take_row(FINAL_GAIN_AT, D)
    final_bias = take_row(FINAL_BIAS_AT, D)
    head_bias = take_row(HEAD_BIAS_AT, HEAD_LANES)

    row_at = (
        (PRE_GAIN_AT, D), (PRE_BIAS_AT, D), (QUERY_BIAS_AT, D), (VALUE_BIAS_AT, D), (PROJ_BIAS_AT, D),
        (MID_GAIN_AT, D), (MID_BIAS_AT, D), (FC1_BIAS_AT, FF), (FC2_BIAS_AT, D),
    )

    def take_layer(n, buf):
        spread(buf, layer_rows)
        take(wqkv.at[n], QKV_AT, D, 3 * D)
        take(wproj.at[n], PROJ_AT, D, D)
        take(wfc1.at[n], FC1_AT, D, FF)
        take(wfc2.at[n], FC2_AT, FF, D)
        for i, (at, width) in enumerate(row_at):
            vecs[n, i : i + 1, :width] = take_row(at, width)

    def vec(n, i):
        return vecs[n, i : i + 1, : row_at[i][1]]

    queue.extend(gather_1.steps())
    gather_0.last()
    pump(1)
    gather_0.finish()
    take_layer(0, b0)

    def tile_rows(i):
        return pl.ds(pl.multiple_of(i * ROWS, ROWS), ROWS)

    def onehot_of(place):
        iota = lax.broadcasted_iota(jnp.int32, (1, wpos.shape[0]), 1).astype(FULL)
        return (place == iota).astype(LOW)

    def embed(i, carry):
        r = tile_rows(i)
        place = pos_col[r, 0:1]
        pixel = dot(pat[r, :], wpat[...]) + patch_bias
        stream = dot(onehot_of(place), wpos[...]) + jnp.where(place < TABLE, pixel, 0.0)
        x0[r, :] = stream
        unit, inverse = normalise(stream)
        unit_a[r, :] = unit
        inv_a[r, :] = jnp.broadcast_to(inverse, (ROWS, LANES))
        h = (unit * vec(0, 0) + vec(0, 1)).astype(LOW)
        h_a[r, :] = h
        bias = jnp.concatenate([vec(0, 2), jnp.zeros((1, D), FULL), vec(0, 3)], axis=1)
        qkv[r, :] = (dot(h, wqkv[0]) + bias).astype(LOW)
        return carry

    lax.fori_loop(0, SEQ // ROWS, embed, 0)

    def window_rows(j):
        start = jnp.minimum((102 * j) // 16 * 16, SEQ - WINDOW)
        return pl.ds(pl.multiple_of(start, 16), WINDOW)

    def both(x):
        zero = jnp.zeros_like(x)
        return jnp.concatenate([jnp.where(head_of_lane == 0, x, zero), jnp.where(head_of_lane == 1, x, zero)], axis=0)

    def merge(x):
        return jnp.where(head_of_lane == 0, x[:WINDOW], x[WINDOW:])

    attl[...] = jnp.zeros_like(attl)

    def window_masks(j, r):
        own = seg_col[r, :]
        first = (2 * j).astype(FULL)
        mine = (own >= first) & (own < first + 2.0)
        other = jnp.transpose(jnp.where(mine, own, -1.0))
        pair = jnp.concatenate([own, own], axis=1) == jnp.concatenate([other, other], axis=1)
        return mine, pair

    def keep_own(mine, ref, r, lanes, value):
        ref[r, lanes] = jnp.where(mine, value, ref[r, lanes].astype(FULL)).astype(LOW)

    def attend(j, carry):
        r = window_rows(j)
        mine, pair = window_masks(j, r)
        for g in range(HEADS // 2):
            lanes = slice(g * LANES, (g + 1) * LANES)
            q2 = both(qkv[r, lanes])
            keys = qkv[r, D + g * LANES : D + (g + 1) * LANES]
            values = qkv[r, 2 * D + g * LANES : 2 * D + (g + 1) * LANES]
            scores = jnp.where(pair, dot_nt(keys, q2) * SCORE_SCALE, MASK_FILL)
            e = jnp.exp(scores - jnp.max(scores, axis=0, keepdims=True))
            p = jnp.where(pair, e * (1.0 / jnp.sum(e, axis=0, keepdims=True)), 0.0).astype(LOW)
            probs[j, g] = p
            keep_own(mine, attl, r, lanes, merge(dot_tn(p, values)))
        return carry

    for half in range(2):
        lax.fori_loop(half * WINDOWS // 2, (half + 1) * WINDOWS // 2, attend, 0)
        pump(2)

    def feed(i, carry):
        r = tile_rows(i)
        middle = x0[r, :] + dot(attl[r, :], wproj[0]) + vec(0, 4)
        unit, inverse = normalise(middle)
        unit_b[r, :] = unit
        inv_b[r, :] = jnp.broadcast_to(inverse, (ROWS, LANES))
        h = (unit * vec(0, 5) + vec(0, 6)).astype(LOW)
        h_b[r, :] = h
        for c in range(4):
            lanes = slice(c * D, (c + 1) * D)
            value, steep = gelu_parts(dot(h, wfc1[0, :, lanes]) + vecs[0, 7:8, lanes])
            act[r, lanes] = value.astype(LOW)
            slope[r, lanes] = steep.astype(LOW)
        x1[r, :] = middle + dot(act[r, :], wfc2[0]) + vec(0, 8)
        return carry

    lax.fori_loop(0, SEQ // ROWS, feed, 0)

    pump(99)
    gather_1.last()
    gather_1.finish()
    take_layer(1, b1)
    unit_c = x0
    h_c = low

    def kv_rows(i, carry):
        r = tile_rows(i)
        unit, inverse = normalise(x1[r, :])
        unit_c[r, :] = unit
        inv_c[r, :] = jnp.broadcast_to(inverse, (ROWS, LANES))
        h = (unit * vec(1, 0) + vec(1, 1)).astype(LOW)
        h_c[r, :] = h
        bias = jnp.concatenate([jnp.zeros((1, D), FULL), vec(1, 3)], axis=1)
        kv[r, :] = (dot(h, wqkv[1, :, D:]) + bias).astype(LOW)
        return carry

    lax.fori_loop(0, SEQ // ROWS, kv_rows, 0)

    h_s = dot(picker_low, h_c[...]).astype(LOW)
    x_s = sum(dot(picker_low, part) for part in exact_parts(x1[...]))
    q_s = (dot(h_s, wqkv[1, :, :D]) + vec(1, 2)).astype(LOW)
    stack_rows = lax.broadcasted_iota(jnp.int32, (HEADS * PICKED, 1), 0)
    stack_lanes = lax.broadcasted_iota(jnp.int32, (1, D), 1)
    own_head = (stack_rows // PICKED) == (stack_lanes // HEAD_DIM)

    def stack(x):
        tall = jnp.concatenate([x.astype(FULL)] * HEADS, axis=0)
        return jnp.where(own_head, tall, 0.0).astype(LOW)

    def unstack(x):
        x = jnp.where(own_head, x, 0.0)
        total = x[:PICKED]
        for h in range(1, HEADS):
            total += x[h * PICKED : (h + 1) * PICKED]
        return total

    q6 = stack(q_s)
    image6 = jnp.concatenate([picked_image] * HEADS, axis=0)
    mask6 = image6 == seg_row
    scores = jnp.where(mask6, dot_nt(q6, kv[:, :D]) * SCORE_SCALE, MASK_FILL)
    e = jnp.exp(scores - jnp.max(scores, axis=-1, keepdims=True))
    p6 = e / jnp.sum(e, axis=-1, keepdims=True)
    p6_low = p6.astype(LOW)
    att_s = unstack(dot(p6_low, kv[:, D:])).astype(LOW)
    mid_s = x_s + dot(att_s, wproj[1]) + vec(1, 4)
    unit_m, inv_m = normalise(mid_s)
    h2_s = (unit_m * vec(1, 5) + vec(1, 6)).astype(LOW)
    act_s, steep_s = gelu_parts(dot(h2_s, wfc1[1]) + vec(1, 7))
    act_s = act_s.astype(LOW)
    x2_s = mid_s + dot(act_s, wfc2[1]) + vec(1, 8)

    unit_f, inv_f = normalise(x2_s)
    summary = (unit_f * final_gain + final_bias).astype(LOW)
    arranged = dot(summary, arrange[...]).astype(LOW)
    logits = head_bias
    spans = []
    for k in range(GROUP):
        at = 2 * CLASSES * k
        block, shift = at // LANES, at % LANES
        blocks = (at + 2 * CLASSES - 1) // LANES - block + 1
        spans.append((block, shift, blocks))
        s_k = arranged[:, k * LANES : k * LANES + GROUPS]
        wide = (HEAD_LANES // LANES + 1) * LANES
        part = dot(s_k, whead[:, block * LANES : block * LANES + wide])
        if shift:
            part = pltpu.roll(part, wide - shift, 1)
        logits = logits + part[:, :HEAD_LANES]
    column = lax.broadcasted_iota(jnp.int32, (PICKED, HEAD_LANES), 1)
    second = picked_row >= IMAGES
    low_end = jnp.where(second, CLASSES, 0)
    valid = (column >= low_end) & (column < low_end + CLASSES)
    live = picked_row < 2 * IMAGES
    target = jnp.zeros((PICKED, 1), jnp.int32)
    for i in range(IMAGES):
        target = jnp.where(picked_row == i, lab[0, i], target)
        target = jnp.where(picked_row == IMAGES + i, CLASSES + tea[0, i], target)
    hit = column == target
    logits = jnp.where(valid, logits, -3e38)
    top = jnp.max(logits, axis=-1, keepdims=True)
    e = jnp.exp(logits - top)
    total = jnp.sum(e, axis=-1, keepdims=True)
    hit_logit = jnp.sum(jnp.where(hit, logits, 0.0), axis=-1, keepdims=True)
    each = jnp.where(live, top + jnp.log(total) - hit_logit, 0.0)
    loss_sum = jnp.sum(each, axis=0, keepdims=True)
    grad_logits = jnp.where(live, (e / total - hit.astype(FULL)) * loss_scale, 0.0)
    grad_low = grad_logits.astype(LOW)
    grad_wide = jnp.concatenate([grad_low.astype(FULL), jnp.zeros((PICKED, LANES), FULL)], axis=1)

    grad_arranged = []
    for k, (block, shift, blocks) in enumerate(spans):
        turned = (pltpu.roll(grad_wide, shift, 1) if shift else grad_wide).astype(LOW)
        turned = turned[:, : blocks * LANES]
        s_k = arranged[:, k * LANES : k * LANES + GROUPS]
        grad_w = dot_tn(s_k, turned)
        for j in range(blocks):
            rows = pl.ds(HEAD_AT + block + j, GROUPS, stride=GROUP_ROWS)
            piece = grad_w[:, j * LANES : (j + 1) * LANES]
            if k and j == 0:
                piece = piece + flat[rows, :]
            flat[rows, :] = piece
        back = dot_nt(turned, whead[:, block * LANES : (block + blocks) * LANES])
        grad_arranged.append(jnp.concatenate([back, jnp.zeros((PICKED, LANES - GROUPS), FULL)], axis=1))
    parts = jnp.concatenate(exact_parts(jnp.concatenate(grad_arranged, axis=1)), axis=0)
    parts = dot_nt(parts, arrange[...])
    grad_summary = parts[:PICKED] + parts[PICKED : 2 * PICKED] + parts[2 * PICKED :]
    put_row(HEAD_BIAS_AT, col_sum(grad_low))
    put_row(FINAL_GAIN_AT, col_sum(grad_summary * unit_f))
    put_row(FINAL_BIAS_AT, col_sum(grad_summary))
    flat[GLOBAL_END:GLOBAL_ALL, :] = jnp.zeros((GLOBAL_ALL - GLOBAL_END, LANES), FULL)
    for gather in gathers:
        gather.drain()
    border = FINAL_GAIN_AT // global_rows
    gather_rows(bg, global_rows, border + 1)
    kept = (border + 1) * global_rows - FINAL_GAIN_AT
    edge[:kept, :] = flat[FINAL_GAIN_AT : FINAL_GAIN_AT + kept, :]
    dx_s = norm_back(grad_summary, final_gain, unit_f, inv_f)

    out_s = dx_s.astype(LOW)
    for c in range(4):
        put(FC2_AT, c * D, D, dot_tn(act_s[:, c * D : (c + 1) * D], out_s))
    put_row(FC2_BIAS_AT, col_sum(out_s))
    gpre_s = (dot_nt(out_s, wfc2[1]) * steep_s).astype(LOW)
    put(FC1_AT, 0, FF, dot_tn(h2_s, gpre_s))
    put_row(FC1_BIAS_AT, col_sum(gpre_s))
    gh2_s = dot_nt(gpre_s, wfc1[1])
    put_row(MID_GAIN_AT, col_sum(gh2_s * unit_m))
    put_row(MID_BIAS_AT, col_sum(gh2_s))
    gmid_s = dx_s + norm_back(gh2_s, vec(1, 5), unit_m, inv_m)
    gmid_low = gmid_s.astype(LOW)
    put(PROJ_AT, 0, D, dot_tn(att_s, gmid_low))
    put_row(PROJ_BIAS_AT, col_sum(gmid_low))
    gatt6 = stack(dot_nt(gmid_low, wproj[1]).astype(LOW))
    gprob = dot_nt(gatt6, kv[:, D:])
    gscore = (p6 * (gprob - jnp.sum(p6 * gprob, axis=-1, keepdims=True))).astype(LOW)
    gq_s = (unstack(dot(gscore, kv[:, :D])) * SCORE_SCALE).astype(LOW)
    gkeys = (dot_tn(gscore, q6) * SCORE_SCALE).astype(LOW)
    gvalues = dot_tn(p6_low, gatt6).astype(LOW)
    put_row(QUERY_BIAS_AT, col_sum(gq_s))
    put_row(VALUE_BIAS_AT, col_sum(gvalues))
    kv[:, :D] = gkeys
    kv[:, D:] = gvalues
    put(QKV_AT, 0, 3 * D, dot_tn(h_s, gq_s))
    put(QKV_AT, 0, 3 * D, dot_tn(h_c[...], kv[:, :D]), 3)
    put(QKV_AT, 0, 3 * D, dot_tn(h_c[...], kv[:, D:]), 6)
    back_s = jnp.concatenate([dot_nt(gq_s, wqkv[1, :, :D]), gmid_s], axis=1)

    back_parts = jnp.concatenate(exact_parts(back_s), axis=0)
    dx = x1

    def kv_back(i, carry):
        gain_sum, bias_sum = carry
        r = tile_rows(i)
        image_col = seg_col[r, 0:1]
        place_col = pos_col[r, 0:1]
        lane = lax.broadcasted_iota(jnp.int32, (1, PICKED), 1).astype(FULL)
        lane_image = jnp.where(lane < IMAGES, lane, lane - IMAGES)
        lane_place = jnp.where(lane < IMAGES, float(TABLE), TABLE + 1.0)
        back_pick = (
            (image_col == lane_image) & (place_col == lane_place) & (lane < 2.0 * IMAGES)
        ).astype(LOW)
        back = dot(jnp.concatenate([back_pick] * 3, axis=1), back_parts)
        grad = back[:, :D] + dot_nt(kv[r, :], wqkv[1, :, D:])
        unit = unit_c[r, :]
        dx[r, :] = back[:, D:] + norm_back(grad, vec(1, 0), unit, inv_c[r, 0:1])
        return gain_sum + col_sum(grad * unit), bias_sum + col_sum(grad)

    zero_row = jnp.zeros((1, D), FULL)
    gain_sum, bias_sum = lax.fori_loop(0, SEQ // ROWS, kv_back, (zero_row, zero_row))
    put_row(PRE_GAIN_AT, gain_sum)
    put_row(PRE_BIAS_AT, bias_sum)
    flat[LAYER_END:, :] = jnp.zeros((LAYER_ALL - LAYER_END, LANES), FULL)
    gather_rows(b1, layer_rows)
    scatter_1 = Scatter(place, b1, r1c, r1q, r1p, r1z, s1, sends.at[3], scatter_recv.at[0])
    queue.extend(scatter_1.steps())
    pump(1)

    def feed_back(i, carry):
        fc1_sum, fc2_sum, proj_sum, gain_sum, bias_sum = carry
        r = tile_rows(i)
        grad_out = dx[r, :]
        out_low = grad_out.astype(LOW)
        low[r, :] = out_low
        for c in range(4):
            lanes = slice(c * D, (c + 1) * D)
            slope[r, lanes] = (dot_nt(out_low, wfc2[0, lanes, :]) * slope[r, lanes].astype(FULL)).astype(LOW)
        grad_h = dot_nt(slope[r, :], wfc1[0])
        unit = unit_b[r, :]
        middle = grad_out + norm_back(grad_h, vec(0, 5), unit, inv_b[r, 0:1])
        dx[r, :] = middle
        middle_low = middle.astype(LOW)
        h2low[r, :] = middle_low
        gatt[r, :] = dot_nt(middle_low, wproj[0]).astype(LOW)
        return (
            fc1_sum + col_sum(slope[r, :]), fc2_sum + col_sum(out_low), proj_sum + col_sum(middle_low),
            gain_sum + col_sum(grad_h * unit), bias_sum + col_sum(grad_h),
        )

    h2low = kv.at[:, 0:D]
    gatt = kv.at[:, D : 2 * D]
    sums = lax.fori_loop(0, SEQ // ROWS, feed_back, (jnp.zeros((1, FF), FULL),) + (zero_row,) * 4)
    pump(3)
    for at, value in zip((FC1_BIAS_AT, FC2_BIAS_AT, PROJ_BIAS_AT, MID_GAIN_AT, MID_BIAS_AT), sums):
        put_row(at, value)

    for c in range(4):
        lanes = slice(c * D, (c + 1) * D)
        put(FC2_AT, c * D, D, dot_tn(act[:, lanes], low[...]))
        put(FC1_AT, 0, FF, dot_tn(h_b[...], slope[:, lanes]), 3 * c)
    put(PROJ_AT, 0, D, dot_tn(attl[...], h2low[...]))

    pump(2)

    def attend_back(j, carry):
        r = window_rows(j)
        mine, _ = window_masks(j, r)
        for g in range(HEADS // 2):
            lanes = slice(g * LANES, (g + 1) * LANES)
            key_lanes = slice(D + g * LANES, D + (g + 1) * LANES)
            value_lanes = slice(2 * D + g * LANES, 2 * D + (g + 1) * LANES)
            q2 = both(qkv[r, lanes])
            go2 = both(gatt[r, lanes])
            keys = qkv[r, key_lanes]
            p_low = probs[j, g]
            p = p_low.astype(FULL)
            gp = dot_nt(qkv[r, value_lanes], go2)
            gs = (p * (gp - jnp.sum(p * gp, axis=0, keepdims=True))).astype(LOW)
            keep_own(mine, qkv, r, lanes, merge(dot_tn(gs, keys)) * SCORE_SCALE)
            keep_own(mine, qkv, r, key_lanes, dot(gs, q2) * SCORE_SCALE)
            keep_own(mine, qkv, r, value_lanes, dot(p_low, go2))
        return carry

    for half in range(2):
        lax.fori_loop(half * WINDOWS // 2, (half + 1) * WINDOWS // 2, attend_back, 0)
        pump(2)

    def qkv_back(i, carry):
        query_sum, value_sum, gain_sum, bias_sum, embed_sum = carry
        r = tile_rows(i)
        held = seg_col[r, 0:1] < float(IMAGES)
        grads = jnp.where(held, qkv[r, :].astype(FULL), 0.0)
        gq, gv = grads[:, :D], grads[:, 2 * D :]
        qkv[r, :] = grads.astype(LOW)
        grad = dot_nt(qkv[r, :], wqkv[0])
        unit = unit_a[r, :]
        full = dx[r, :] + norm_back(grad, vec(0, 0), unit, inv_a[r, 0:1])
        dx[r, :] = full
        place = pos_col[r, 0:1]
        pixel = jnp.where(place < TABLE, full, 0.0).astype(LOW)
        low[r, :] = pixel
        return (
            query_sum + col_sum(gq), value_sum + col_sum(gv), gain_sum + col_sum(grad * unit),
            bias_sum + col_sum(grad), embed_sum + col_sum(pixel),
        )

    sums = lax.fori_loop(0, SEQ // ROWS, qkv_back, (zero_row,) * 5)
    for at, value in zip((QUERY_BIAS_AT, VALUE_BIAS_AT, PRE_GAIN_AT, PRE_BIAS_AT), sums):
        put_row(at, value)
    for c in range(3):
        put(QKV_AT, 0, 3 * D, dot_tn(h_a[...], qkv[:, c * D : (c + 1) * D]), 3 * c)
    pump(99)
    gather_rows(b0, layer_rows)
    scatter_0 = Scatter(place, b0, r0c, r0q, r0p, r0z, s0, sends.at[4], scatter_recv.at[1])
    queue.extend(scatter_0.steps())
    pump(1)

    for c in range(2):
        put(PATCH_AT, c * D, D, dot_tn(pat[:, c * D : (c + 1) * D], low[...]))
    place_col = pos_col[:, 0:1]
    onehot = onehot_of(place_col)
    high = dx[...].astype(LOW)
    rest = (dx[...] - high.astype(FULL)).astype(LOW)
    table = dot_tn(onehot, high) + dot_tn(onehot, rest)
    put(POS_AT, 0, D, table[: TABLE + 2])
    put_row(PATCH_BIAS_AT, sums[4])
    flat[FINAL_GAIN_AT : FINAL_GAIN_AT + kept, :] = edge[:kept, :]
    gather_rows(bg, global_rows, 0, border + 1)
    scatter_g = Scatter(place, bg, rgc, rgq, rgp, rgz, sg, sends.at[5], scatter_recv.at[2])
    steps_0, steps_g = queue, scatter_g.steps()
    steps_g.pop(0)()
    queue = []
    while steps_0 or steps_g:
        for steps in (steps_0, steps_g):
            if steps:
                steps.pop(0)()

    squares = jnp.zeros((1, 1), FULL)
    for s, rows in ((s0, layer_rows), (s1, layer_rows), (sg, global_rows)):
        used = s[:rows, :]
        squares += jnp.sum(jnp.sum(used * used, axis=0, keepdims=True), axis=1, keepdims=True)
    row = lax.broadcasted_iota(jnp.int32, (8, LANES), 0)
    tile = jnp.where(row == 0, squares, loss_sum)
    shared[...] = add_over_slice(place, tile, tiles, tile_send, tile_recv)
    for scatter in (scatter_1, scatter_0, scatter_g):
        scatter.drain()


def padded(rows):
    return rows + -rows % 16


def step_call(place, loss_scale, pat, pos, seg, lab, tea, lm, gm):
    vmem = pl.BlockSpec(memory_space=pltpu.VMEM)
    smem = pl.BlockSpec(memory_space=pltpu.SMEM)
    n, nz = place.n, place.nz
    rows = padded(lm.shape[1]), padded(lm.shape[1]), padded(gm.shape[0])

    def shape(*dims, kind=FULL):
        return pltpu.VMEM(dims, kind)

    def low(*dims):
        return pltpu.VMEM(dims, LOW)

    scratch = [low(n, 2, nz, n, r, LANES) for r in rows]
    for r in rows:
        scratch += [
            low(n, nz, n, r, LANES), low(n - 1, n, nz, r, LANES), low(n - 1, nz, r, LANES), low(nz - 1, r, LANES)
        ]
    tiles = 2 + 2 * n + nz
    scratch += [
        shape(LAYER_ALL, LANES), shape(gm.shape[0] + 8, LANES), shape(rows[0], LANES), low(D, GROUP * LANES),
        low(2, D, 3 * D), low(2, D, D), low(2, D, FF), low(2, FF, D),
        low(PATCH, D), low(256, D), low(GROUPS, (GROUP_ROWS + 1) * LANES),
        shape(2, 16, FF),
        shape(SEQ, LANES), shape(SEQ, LANES),
        shape(SEQ, D), shape(SEQ, LANES), low(SEQ, D),
        shape(SEQ, D), shape(SEQ, LANES), low(SEQ, D),
        low(SEQ, 3 * D), low(WINDOWS, HEADS // 2, WINDOW, 2 * WINDOW),
        low(SEQ, D), shape(SEQ, D), shape(SEQ, D),
        low(SEQ, FF), low(SEQ, FF), low(SEQ, 2 * D), low(SEQ, D), shape(SEQ, LANES),
        shape(tiles, 8, LANES),
        pltpu.SemaphoreType.DMA((6,)),
        pltpu.SemaphoreType.DMA((3, nz + nz * n + 2 * n)), pltpu.SemaphoreType.DMA((3, 2 * n + n * n + nz)),
        pltpu.SemaphoreType.DMA((tiles,)), pltpu.SemaphoreType.DMA((tiles,)),
    ]
    return pl.pallas_call(
        functools.partial(step_kernel, place, loss_scale),
        out_shape=[jax.ShapeDtypeStruct((r, LANES), FULL) for r in rows] + [jax.ShapeDtypeStruct((8, LANES), FULL)],
        in_specs=[vmem] * 3 + [smem] * 2 + [vmem] * 2,
        out_specs=[vmem] * 4,
        scratch_shapes=scratch,
        compiler_params=pltpu.CompilerParams(collective_id=0, has_side_effects=True, vmem_limit_bytes=VMEM_BYTES),
    )(pat, pos, seg, lab, tea, lm, gm)

def adam(master, moment, second, gradient, factor):
    clipped = gradient * factor
    new_moment = BETA_ONE * moment + (1.0 - BETA_ONE) * clipped
    new_second = BETA_TWO * second + (1.0 - BETA_TWO) * clipped * clipped
    fix_one = 1.0 - BETA_ONE**STEP
    fix_two = 1.0 - BETA_TWO**STEP
    update = new_moment / fix_one / (jnp.sqrt(new_second / fix_two) + ADAM_EPS) + WEIGHT_DECAY * master
    return master - LEARN_RATE * update, new_moment, new_second


def shards(sizes, pat, pos, seg, lab, tea, lm, lo, ls, gm, go, gs):
    place = Place(sizes)
    rows, global_rows = lm.shape[1] // LANES, gm.shape[0] // LANES
    loss_scale = 1.0 / (2 * IMAGES * sizes[0] * sizes[1])
    assert pat.shape[0] == 1 and (lm.shape[1], gm.shape[0]) == (rows * LANES, global_rows * LANES)
    assert sizes[0] * sizes[1] * rows == LAYER_ALL and sizes[0] * sizes[1] * global_rows == GLOBAL_ALL
    s0, s1, sg, total = step_call(
        place, loss_scale, pat[0], pos, seg, lab, tea,
        lm.reshape(2, rows, LANES), gm.reshape(global_rows, LANES),
    )
    layer = jnp.stack([s0[:rows].reshape(-1), s1[:rows].reshape(-1)])
    gg = sg[:global_rows].reshape(-1)
    norm = jnp.sqrt(total[0, 0])
    factor = jnp.minimum(1.0, CLIP_NORM / norm)
    return adam(lm, lo, ls, layer, factor) + adam(gm, go, gs, gg, factor) + (norm, total[1, 0])


def solution(mesh):
    axes = tuple(mesh.axis_names)
    split = P(axes)
    wide = P(None, axes)
    return jax.shard_map(
        functools.partial(shards, tuple(mesh.shape[a] for a in axes)),
        mesh=mesh,
        in_specs=(split,) * 5 + (wide,) * 3 + (split,) * 3,
        out_specs=(wide,) * 3 + (split,) * 3 + (P(), P()),
        check_vma=False,
    )
```

time: 202 us -> 189 us (0.936)
  Pallas kernels: 189 us -> 176 us
    pallas_call x3 -> x1, Pallas kernels: 189 us -> 176 us  [step_call(): pl.pallas_call(functools.partial(step_kernel, place, loss_scale), out_sha...]
where the time goes in v1:
time: 189 us
  Pallas kernels  176 us (93%)
  local copies, waits for them, and re-layouts  5.03 us (3%)
  other arithmetic  4.76 us (3%)
  between operations  2.59 us (1%)
    pallas_call x1, Pallas kernels, step_call(): pl.pallas_call(functools.partial(step_kernel, place, loss_scale), out_sha...  176 us
    sub x2, other arithmetic, adam(): return (master - LEARN_RATE * update, new_moment, new_second)  4.76 us

profile of v1, /device:TPU:0, one launch (start us, length us, event | category | flops | bytes accessed | tf_op | source)
XLA Modules:
  0.0 188.5 jit_solution(15615095609008239406)
XLA Ops:
  0.6 1.8 copy.21
  2.4 176.2 %shard_map.170 = (f32[448,128]{1,0:T(8,128)}, f32[448,128]{1,0:T(8,128)}, f32[288,128]{1,0:T(8,128)}, f32[8,128]{1,0:T(8,128)}) custom-call(bf16[768,768]{1,0:T(8,128)(2,1)} %bitcast.19, s32[1,768]{1,0:T(1,128)} %pos.1, s32[1,768]{1,0:T(1,128)} %seg.1, s32[1,15]{1,0:T(1,128)} %lab.1, s32[1,15]{1,0:T(1,128)} %tea.1, f32[2,440,128]{2,1,0:T(8,128)} %bitcast.17, ...), custom_call_target="tpu_custom_call" | custom-call | tf_op jit(solution)/shard_map/pallas_call | solution.py:962
  178.6 0.0 copy-start
  178.6 0.0 copy-start.2
  178.6 1.3 fusion.6
  180.6 1.0 slice.15
  181.6 1.0 slice.16
  182.6 0.0 copy-done
  182.6 0.0 copy-done.2
  182.6 0.0 copy-start.1
  182.6 0.0 copy-start.3
  182.6 0.0 copy-start.4
  182.6 0.0 copy-start.5
  182.6 3.9 %multiply_subtract_fusion = (f32[2,56320]{1,0:T(2,128)}, f32[2,56320]{1,0:T(2,128)}, f32[2,56320]{1,0:T(2,128)}) fusion(f32[2,56320]{1,0:T(2,128)S(1)} %copy-done, f32[]{:T(128)S(6)} %min_shard_map.3, f32[1,56320]{1,0:T(1,128)S(1)} %bitcast.21, f32[1,56320]{1,0:T(1,128)S(1)} %bitcast.20, f32[2,56320]{1,0:T(2,128)S(1)} %copy-done.2, f32[2,56320]{1,0:T(2,128)} %param.18), kind=kLoop, calls=%fused_computation.4 | loop fusion | flops 1914880 | bytes 3153924 | tf_op jit(solution)/shard_map/sub | solution.py:978
  186.6 0.0 copy-done.1
  186.6 0.0 copy-done.3
  186.6 0.0 copy-done.4
  186.6 0.0 copy-done.5
  186.6 0.8 multiply_subtract_fusion.1
Async XLA Ops:
  178.6 4.0 %copy-start = (f32[2,56320]{1,0:T(2,128)S(1)}, f32[2,56320]{1,0:T(2,128)}, u32[]{:S(2)}) copy-start(f32[2,56320]{1,0:T(2,128)} %param.16) | copy-start | bytes 1351684
  178.6 3.9 %copy-start.2 = (f32[2,56320]{1,0:T(2,128)S(1)}, f32[2,56320]{1,0:T(2,128)}, u32[]{:S(2)}) copy-start(f32[2,56320]{1,0:T(2,128)} %param.17) | copy-start | bytes 1351684
  182.6 4.0 %copy-start.1 = (f32[35840]{0:T(1024)S(1)}, f32[35840]{0:T(1024)}, u32[]{:S(2)}) copy-start(f32[35840]{0:T(1024)} %param.19) | copy-start | bytes 430084
  182.6 4.0 %copy-start.3 = (f32[35840]{0:T(1024)S(1)}, f32[35840]{0:T(1024)}, u32[]{:S(2)}) copy-start(f32[35840]{0:T(1024)} %param.20) | copy-start | bytes 430084
  182.6 4.0 %copy-start.4 = (f32[35840]{0:T(1024)S(1)}, f32[35840]{0:T(1024)}, u32[]{:S(2)}) copy-start(f32[35840]{0:T(1024)} %param.21) | copy-start | bytes 430084
  182.6 4.0 %copy-start.5 = (f32[288,128]{1,0:T(8,128)S(1)}, f32[288,128]{1,0:T(8,128)}, u32[]{:S(2)}) copy-start(f32[288,128]{1,0:T(8,128)} %get-tuple-element.15) | copy-start | bytes 442372
